TPU v7x, 256 devices: a whole 4x4x8 slice. The times are simulated.
256 devices in a mesh: seq: 32 (over x, z), head: 8 (over y, core).
Axes of the slice: x: 4, y: 4, z: 8, core: 2. Of those that a mesh axis runs over, the one named last changes fastest.
Arguments:
- x_in: bfloat16 [16384, 8192], P('seq', 'head'), may hold values from -1.5 to 1.5
- z_in: bfloat16 [16384, 8192], P('seq', 'head'), may hold values from -6 to 6
- bc_in: bfloat16 [16384, 8, 2, 128], P('seq', 'head'), may hold values from -3 to 3
- dt_raw: float32 [16384, 128], P('seq', 'head'), may hold values from -4 to 1000
- dt_bias: float32 [128], P('head'), may hold values from -5 to 1.5
- a_log: float32 [128], P('head'), may hold values from -8 to -2
- conv_x: bfloat16 [4, 8192], P(None, 'head'), may hold values from -3 to 3
- conv_bc: bfloat16 [4, 8, 2, 128], P(None, 'head'), may hold values from -3 to 3
- skip_gain: float32 [128], P('head'), may hold values from 0.5 to 2
- norm_gain: bfloat16 [8192], P('head'), may hold values from 0.099609375 to 1.8984375
- score_weight: bfloat16 [8192], P('head'), may hold values from -0.25 to 0.25
- passage_ids: int32 [16384], P('seq'), may hold values from 0 to 99, as said below
- teacher_logits: float32 [100], replicated, may hold values from -12 to 12
- teacher_order: int32 [100], replicated, may hold values from 0 to 99, each once
Outputs:
- mixed_out: bfloat16 [16384, 8192], P('seq', 'head')
- token_grad: float32 [16384], P('seq')
- kl_loss: float32 [], replicated
Inputs may be any that keep to these rules, and one draw needn't show every extreme that they name: `passage_ids`: never falls along the tokens; each of the 100 passages has at least one token and at most 491, and one has exactly that many. Each passage appears once; teacher_logits[r] is the teacher's logit of passage teacher_order[r].
All inputs are finite; a program needn't handle non-finite values.
Results may differ from a plain program's by a relative error of at most 0.0051.
Values may be sent and summed in bfloat16 or wider, within the bound.
A program may use at most 128 MiB of HBM per device.

v0:
```python
from functools import partial

import jax
import jax.numpy as jnp
from jax import lax
from jax.sharding import PartitionSpec as P

CH = 128
NP = 100


EPS = 1e-05
CAP = 8.0


def from_behind(block, axis, distance):
    devices = range(lax.axis_size(axis))
    route = [(i - distance, i) for i in devices if i - distance in devices]
    return lax.ppermute(block, axis, route)


def entering_2(value, axis, join, neutral):
    count, mine = (lax.axis_size(axis), lax.axis_index(axis))
    pieces = jax.tree.map(lambda part: lax.all_gather(part, axis), value)
    subtotal = jax.tree.map(
        lambda part, zero: jnp.full_like(part, 0) + jnp.asarray(zero, part.dtype), value, neutral
    )

    def hop(position, subtotal):
        longer = join(subtotal, jax.tree.map(lambda part: part[position], pieces))
        return jax.tree.map(lambda new, old: jnp.where(position < mine, new, old), longer, subtotal)

    return lax.fori_loop(0, count - 1, hop, subtotal)


def convolve(stream, tail, kernel):
    length = stream.shape[0]
    padded = jnp.concatenate([tail, stream], axis=0)
    total = jnp.zeros(stream.shape, jnp.float32)
    for tap in range(kernel.shape[0]):
        total = total + padded[tap : tap + length].astype(jnp.float32) * kernel[tap].astype(
            jnp.float32
        )
    return jax.nn.silu(total).astype(jnp.bfloat16)


def block_terms(inputs, bmat, cmat, steps, rates, per_group):
    length = inputs.shape[0]
    cumul = jnp.cumsum(rates, axis=0)
    pairs = jnp.einsum("tgn,sgn->gts", cmat, bmat, preferred_element_type=jnp.float32)
    pairs = jnp.repeat(pairs, per_group, axis=0)
    rows = lax.broadcasted_iota(jnp.int32, (length, length), 0)
    cols = lax.broadcasted_iota(jnp.int32, (length, length), 1)
    lower = (rows >= cols)[None]
    across = cumul.T
    gap = jnp.where(lower, across[:, :, None] - across[:, None, :], 0.0)
    scale_multiplier = jnp.where(lower, jnp.exp(gap), 0.0)
    weight_values = (pairs * scale_multiplier * steps.T[:, None, :]).astype(jnp.bfloat16)
    inner = jnp.einsum("hts,shp->thp", weight_values, inputs, preferred_element_type=jnp.float32)
    tail_scale = jnp.exp(cumul[-1][None, :] - cumul) * steps
    loaded = (inputs.astype(jnp.float32) * tail_scale[:, :, None]).astype(jnp.bfloat16)
    broadcast_heads = jnp.repeat(bmat, per_group, axis=1)
    added = jnp.einsum("shn,shp->hnp", broadcast_heads, loaded, preferred_element_type=jnp.float32)
    return (inner, added, cumul)


def join(earlier, later):
    return (earlier[0] + later[0], earlier[1] * jnp.exp(later[0])[..., None, None] + later[1])


def per_device(
    x_in,
    z_in,
    bc_in,
    dt_raw,
    dt_bias,
    a_log,
    conv_x,
    conv_bc,
    skip_gain,
    norm_gain,
    score_weight,
    passage_ids,
    teacher_logits,
    teacher_order,
):
    high = lax.Precision.HIGHEST
    width = conv_x.shape[0]
    count_here = x_in.shape[0]
    heads_here = dt_raw.shape[1]
    groups_here = bc_in.shape[1]
    per_group = heads_here // groups_here
    head_size = x_in.shape[1] // heads_here
    state_size = bc_in.shape[3]
    blocks = count_here // CH
    tails = from_behind((x_in[count_here - width + 1 :], bc_in[count_here - width + 1 :]), "seq", 1)
    x_conv = convolve(x_in, tails[0], conv_x)
    bc_conv = convolve(bc_in, tails[1], conv_bc)
    steps = jax.nn.softplus(dt_raw + dt_bias[None, :])
    rates = -jnp.exp(a_log)[None, :] * steps
    inputs = x_conv.reshape(blocks, CH, heads_here, head_size)
    bmat = bc_conv[:, :, 0, :].reshape(blocks, CH, groups_here, state_size)
    cmat = bc_conv[:, :, 1, :].reshape(blocks, CH, groups_here, state_size)
    inner, added, cumul = jax.vmap(partial(block_terms, per_group=per_group))(
        inputs,
        bmat,
        cmat,
        steps.reshape(blocks, CH, heads_here),
        rates.reshape(blocks, CH, heads_here),
    )
    local_log = jnp.zeros((heads_here,), jnp.float32)
    local_state = jnp.zeros((heads_here, state_size, head_size), jnp.float32)
    for block in range(blocks):
        local_state = jnp.exp(cumul[block, -1])[:, None, None] * local_state + added[block]
        local_log = local_log + cumul[block, -1]
    entering = entering_2(
        (local_log, local_state),
        "seq",
        join,
        (jnp.zeros_like(local_log), jnp.zeros_like(local_state)),
    )[1]
    carry = entering
    outputs = []
    for block in range(blocks):
        cheads = jnp.repeat(cmat[block], per_group, axis=1).astype(jnp.float32)
        outer = jnp.einsum("thn,hnp->thp", cheads, carry, precision=high)
        outputs.append(
            inner[block]
            + jnp.exp(cumul[block])[:, :, None] * outer
            + skip_gain[None, :, None] * inputs[block].astype(jnp.float32)
        )
        carry = jnp.exp(cumul[block, -1])[:, None, None] * carry + added[block]
    ssd = jnp.concatenate(outputs, axis=0).reshape(count_here, groups_here, per_group * head_size)
    gated = ssd * jax.nn.silu(z_in.astype(jnp.float32)).reshape(
        count_here, groups_here, per_group * head_size
    )
    power = jnp.mean(gated * gated, axis=2, keepdims=True)
    mixed = (
        (gated * lax.rsqrt(power + EPS)).reshape(count_here, -1) * norm_gain.astype(jnp.float32)
    ).astype(jnp.bfloat16)
    self_readout = jnp.dot(mixed, score_weight, preferred_element_type=jnp.float32)
    labels = jnp.arange(NP, dtype=jnp.int32)
    member = (passage_ids[:, None] == labels[None, :]).astype(jnp.float32)
    readout = lax.psum(self_readout, "head")
    sums, counts = lax.psum(
        (jnp.dot(readout, member, precision=high), jnp.sum(member, axis=0)), "seq"
    )
    means = sums / counts
    squash = jnp.tanh(means / CAP)
    scores = CAP * squash
    student = scores - jnp.log(jnp.sum(jnp.exp(scores)))
    ranks = (teacher_order[:, None] == labels[None, :]).astype(jnp.float32)
    teacher = jnp.dot(teacher_logits, ranks, precision=high)
    teacher = teacher - jnp.log(jnp.sum(jnp.exp(teacher)))
    kl_loss = jnp.sum(jnp.exp(teacher) * (teacher - student))
    total = lax.axis_size("seq") * count_here
    coef = (jnp.exp(student) - jnp.exp(teacher)) * (1.0 - squash * squash) * total / counts
    token_grad = jnp.dot(member, coef, precision=high)
    return (mixed, token_grad, kl_loss)


def solution(mesh):
    placed = (
        P("seq", "head"),
        P("seq", "head"),
        P("seq", "head", None, None),
        P("seq", "head"),
        P("head"),
        P("head"),
        P(None, "head"),
        P(None, "head", None, None),
        P("head"),
        P("head"),
        P("head"),
        P("seq"),
        P(),
        P(),
    )
    return jax.shard_map(
        per_device,
        mesh=mesh,
        in_specs=placed,
        out_specs=(P("seq", "head"), P("seq"), P()),
        check_vma=False,
    )
```

profile of v0, /device:TPU:32, one launch (start us, length us, event | category | flops | bytes accessed | tf_op | source)
XLA Modules:
  0.0 352.3 jit_solution(1870625979904468244)
XLA Ops:
  8.0 3.8 %collective-permute-start = (bf16[3,1024]{1,0:T(4,128)(2,1)S(1)}, bf16[3,1024]{1,0:T(4,128)(2,1)S(1)}, u32[]{:S(2)}, u32[]{:S(2)}) collective-permute-start(bf16[3,1024]{1,0:T(4,128)(2,1)S(1)} %slice.151), channel_id=1, source_target_pairs={{0,8},{8,16},{16,24},{24,32},{32,40},{40,48},{48,56},{56,64},{64,7... | collective-permute-start | bytes 18440 | tf_op jit(solution)/shard_map/ppermute | solution.py:19
  12.9 3.8 %collective-permute-start.1 = (bf16[3,1,2,128]{3,0,2,1:T(4,128)(2,1)S(1)}, bf16[3,1,2,128]{3,0,2,1:T(4,128)(2,1)S(1)}, u32[]{:S(2)}, u32[]{:S(2)}) collective-permute-start(bf16[3,1,2,128]{3,0,2,1:T(4,128)(2,1)S(1)} %slice.198), channel_id=1, source_target_pairs={{0,8},{8,16},{16,24},{24,32},{32,40},{40,48},{48,56},{56,64},{64,7... | collective-permute-start | bytes 4616 | tf_op jit(solution)/shard_map/ppermute | solution.py:19
  22.7 1.5 multiply_convert_fusion.4
  25.0 1.3 multiply_convert_fusion.3
  27.0 1.3 copy-done.1
  30.2 1.7 copy.93
  32.5 1.5 copy.95
  34.0 1.5 copy.101
  35.5 1.5 copy.104
  37.9 1.3 convert_element_type.126
  39.9 2.0 exponential_reduce_fusion
  42.6 42.2 %all-gather = f32[32,1,16]{2,1,0:T(1,128)} all-gather(f32[1,1,16]{2,1,0:T(1,128)} %get-tuple-element.166), channel_id=2, replica_groups=mesh['seq'=32,'head'=8] {'seq'}, dimensions={0}, use_global_device_ids=true | all-gather | bytes 2112 | tf_op jit(solution)/shard_map/all_gather | solution.py:24
  85.5 1.3 convert_reduce_fusion
  86.8 1.5 slice_bitcast_fusion.7
  88.3 1.8 fusion.69
  90.1 1.4 slice_convert_fusion.3
  91.5 2.2 copy.100
  93.7 2.1 copy.103
  97.0 3.2 fusion.12
  100.2 69.0 %all-gather.3.cloned.1.call-done = f32[32,16,128,64]{2,3,1,0:T(8,128)} async-done(((f32[1,16,128,64]{2,3,1,0:T(8,128)}), f32[32,16,128,64]{2,3,1,0:T(8,128)}) %all-gather.3.cloned.1.call-update) | async-done | bytes 16777232 | tf_op jit(solution)/shard_map/all_gather | solution.py:24
  169.2 74.3 %while.14 = (s32[]{:T(128)}, f32[16,128,64]{2,1,0:T(8,128)S(1)}, s32[]{:T(128)}, f32[32,16]{1,0:T(8,128)}, f32[32,16,128,64]{2,3,1,0:T(8,128)}, /*index=5*/s32[]{:T(128)}, s32[]{:T(128)}) while((s32[]{:T(128)}, f32[16,128,64]{2,1,0:T(8,128)S(1)}, s32[]{:T(128)}, f32[32,16]{1,0:T(8,128)}, f32[32,16,128,64]{2,3,1,0:T(8,128)}, ...), condition=%wide.region_2.3_spmd.clone, body=%wide.region_1.2_spmd.clone.sunk | while | flops 524292 | bytes 3670313 | solution.py:33
  169.2 1.1 constant_dynamic-slice_fusion.2
  174.0 1.1 constant_dynamic-slice_fusion.2
  243.9 1.5 bitcast_add_fusion.3
  245.8 1.1 fusion.24
  247.0 1.2 fusion.23
  248.2 1.2 fusion.20
  249.4 1.2 fusion.17
  250.6 1.5 pad_maximum_fusion
  252.1 2.0 copy.108
  256.5 14.2 %psum.21 = f32[512]{0:T(512)S(1)} all-reduce(f32[512]{0:T(512)S(1)} %bitcast.168), channel_id=1, replica_groups=mesh['seq'=32,'head'=8] {'head'}, use_global_device_ids=true, to_apply=%region_4.5 | all-reduce | flops 512 | bytes 4096 | tf_op jit(solution)/shard_map/psum | solution.py:144
  270.8 71.9 %all-reduce = (f32[100]{0:T(128)S(1)}, f32[100]{0:T(128)S(1)}) all-reduce(f32[100]{0:T(128)S(1)} %copy-done.38, f32[100]{0:T(128)S(1)} %convolution_bitcast_fusion.4), channel_id=1, replica_groups=mesh['seq'=32,'head'=8] {'seq'}, use_global_device_ids=true, to_apply=%region_7.8 | all-reduce | flops 200 | bytes 1600 | tf_op jit(solution)/shard_map/psum | solution.py:145
  (241 shorter events, 91.4 us)
Async XLA Ops:
  7.2 32.8 %copy-start = (f32[100]{0:T(128)S(1)}, f32[100]{0:T(128)}, u32[]{:S(2)}) copy-start(f32[100]{0:T(128)} %param.28) | copy-start | bytes 1204
  7.2 15.5 %copy-start.14 = (bf16[512,1024]{1,0:T(8,128)(2,1)S(1)}, bf16[512,1024]{1,0:T(8,128)(2,1)}, u32[]{:S(2)}) copy-start(bf16[512,1024]{1,0:T(8,128)(2,1)} %param.16) | copy-start | bytes 3145732
  7.2 13.6 %copy-start.34 = (bf16[4,1,2,128]{3,2,1,0:T(2,128)(2,1)S(1)}, bf16[4,1,2,128]{3,2,1,0:T(2,128)(2,1)}, u32[]{:S(2)}) copy-start(bf16[4,1,2,128]{3,2,1,0:T(2,128)(2,1)} %param.23) | copy-start | bytes 6148
  7.2 162.0 %all-gather.3.cloned.1.call-start = ((), (), s32[]{:S(2)}) async-start(), calls=%async_computation | async-start | bytes 17301504 | tf_op jit(solution)/shard_map/all_gather | solution.py:24
  8.0 14.6 %collective-permute-start = (bf16[3,1024]{1,0:T(4,128)(2,1)S(1)}, bf16[3,1024]{1,0:T(4,128)(2,1)S(1)}, u32[]{:S(2)}, u32[]{:S(2)}) collective-permute-start(bf16[3,1024]{1,0:T(4,128)(2,1)S(1)} %slice.151), channel_id=1, source_target_pairs={{0,8},{8,16},{16,24},{24,32},{32,40},{40,48},{48,56},{56,64},{64,7... | collective-permute-start | bytes 18440 | tf_op jit(solution)/shard_map/ppermute | solution.py:19
  12.9 8.7 %collective-permute-start.1 = (bf16[3,1,2,128]{3,0,2,1:T(4,128)(2,1)S(1)}, bf16[3,1,2,128]{3,0,2,1:T(4,128)(2,1)S(1)}, u32[]{:S(2)}, u32[]{:S(2)}) collective-permute-start(bf16[3,1,2,128]{3,0,2,1:T(4,128)(2,1)S(1)} %slice.198), channel_id=1, source_target_pairs={{0,8},{8,16},{16,24},{24,32},{32,40},{40,48},{48,56},{56,64},{64,7... | collective-permute-start | bytes 4616 | tf_op jit(solution)/shard_map/ppermute | solution.py:19
  19.2 7.8 %copy-start.28 = (f32[16]{0:T(128)}, f32[16]{0:T(128)S(1)}, u32[]{:S(2)}) copy-start(f32[16]{0:T(128)S(1)} %get-tuple-element.167) | copy-start | bytes 196
  26.3 2.1 copy-start.31
  26.3 2.1 copy-start.33
  26.3 2.1 copy-start.36
  91.5 4.3 %copy-start.12 = (f32[128,1024]{1,0:T(8,128)S(1)}, f32[128,1024]{1,0:T(8,128)}, u32[]{:S(2)}) copy-start(f32[128,1024]{1,0:T(8,128)} %get-tuple-element.154) | copy-start | bytes 1572868
  91.5 5.2 %copy-start.11 = (f32[128,1024]{1,0:T(8,128)S(1)}, f32[128,1024]{1,0:T(8,128)}, u32[]{:S(2)}) copy-start(f32[128,1024]{1,0:T(8,128)} %get-tuple-element.153) | copy-start | bytes 1572868
  91.5 5.4 %copy-start.15 = (f32[4,128,128]{2,1,0:T(8,128)S(1)}, f32[4,128,128]{2,1,0:T(8,128)}, u32[]{:S(2)}) copy-start(f32[4,128,128]{2,1,0:T(8,128)} %fusion.69) | copy-start | bytes 786436
  91.5 5.5 %copy-start.23 = (f32[4,16,128]{2,1,0:T(8,128)S(1)}, f32[4,16,128]{2,1,0:T(8,128)}, u32[]{:S(2)}) copy-start(f32[4,16,128]{2,1,0:T(8,128)} %copy.90) | copy-start | bytes 98308
  91.5 5.5 %copy-start.24 = (f32[4,16,128]{2,1,0:T(8,128)S(1)}, f32[4,16,128]{2,1,0:T(8,128)}, u32[]{:S(2)}) copy-start(f32[4,16,128]{2,1,0:T(8,128)} %copy.93) | copy-start | bytes 98308
  91.5 5.5 %copy-start.26 = (pred[128,128]{1,0:T(8,128)(4,1)S(1)}, pred[128,128]{1,0:T(8,128)(4,1)}, u32[]{:S(2)}) copy-start(pred[128,128]{1,0:T(8,128)(4,1)} %iota_compare_fusion.3) | copy-start | bytes 49156
  169.2 74.7 %copy-start.30 = (f32[16]{0:T(128)S(1)}, f32[16]{0:T(128)}, u32[]{:S(2)}) copy-start(f32[16]{0:T(128)} %get-tuple-element.164) | copy-start | bytes 196
  169.2 74.7 %copy-start.32 = (f32[16]{0:T(128)S(1)}, f32[16]{0:T(128)}, u32[]{:S(2)}) copy-start(f32[16]{0:T(128)} %get-tuple-element.168) | copy-start | bytes 196
  243.9 3.0 copy-start.2
  243.9 3.0 copy-start.9
  243.9 3.0 copy-start.18
  243.9 3.0 copy-start.21
  245.8 2.4 copy-start.8
  245.8 2.4 copy-start.17
  245.8 2.4 copy-start.20
  247.0 2.4 copy-start.16
  247.0 2.4 copy-start.29
  252.1 2.0 copy-start.4
  255.4 15.3 %copy-start.35 = (s32[512]{0:T(512)S(1)}, s32[512]{0:T(512)}, u32[]{:S(2)}) copy-start(s32[512]{0:T(512)} %param.27) | copy-start | bytes 6148
  255.4 15.5 %copy-start.38 = (f32[100]{0:T(128)S(1)}, f32[100]{0:T(128)}, u32[]{:S(2)}) copy-start(f32[100]{0:T(128)} %convert_reduce_fusion) | copy-start | bytes 1204
  255.4 88.7 %copy-start.37 = (f32[100]{0:T(128)S(1)}, f32[100]{0:T(128)}, u32[]{:S(2)}) copy-start(f32[100]{0:T(128)} %get-tuple-element.180) | copy-start | bytes 1204
  256.1 89.4 %copy-start.3 = (bf16[512,1024]{1,0:T(8,128)(2,1)}, bf16[512,1024]{1,0:T(8,128)(2,1)S(1)}, u32[]{:S(2)}) copy-start(bf16[512,1024]{1,0:T(8,128)(2,1)S(1)} %multiply_convert_fusion.2) | copy-start | bytes 3145732
  (10 other events, 16.3 us)
Sparse Core Ops, SparseCore 0:
  29.6 139.5 all-gather.2
where the time goes:
time: 356 us; the launch traced here: 352 us
  blocking collectives  128 us (36%)
  local copies, waits for them, and re-layouts  90.4 us (25%)
  waiting for transfers between devices  69 us (19%)
  other arithmetic  26.2 us (7%)
  between operations  16 us (4%)
  matrix products  13.6 us (4%)
  starting transfers between devices  7.68 us (2%)
    psum x1, blocking collectives, per_device(): lax.psum((jnp.dot(readout, member, precision=high), jnp.sum(member, axis=...  71.9 us
    all_gather x1, waiting for transfers between devices, entering_2(): pieces = jax.tree.map(lambda part: lax.all_gather(part, axis), value)  69 us
    dynamic_slice x62, local copies, waits for them, and re-layouts, hop(): longer = join(subtotal, jax.tree.map(lambda part: part[position], pieces))  43.9 us
    all_gather x1, blocking collectives, entering_2(): pieces = jax.tree.map(lambda part: lax.all_gather(part, axis), value)  42.2 us
    exp x31, local copies, waits for them, and re-layouts, join(): jnp.exp(later[0])[..., None, None]  21.5 us
    psum x1, blocking collectives, per_device(): readout = lax.psum(self_readout, 'head')  14.2 us
    select_n x31, other arithmetic, hop(): jnp.where(position < mine, new, old)  7.83 us
    ppermute x2, starting transfers between devices, from_behind(): return lax.ppermute(block, axis, route)  7.64 us
  transfers between devices with their start and end apart: 3, of which 1 were waited for; matrix products, arithmetic and copies ran while one was open for 10% of the time, Pallas kernels for 0%

commit v1 on v0

v1 whole, which is shorter than its diff:
```python
import functools

import jax
import jax.numpy as jnp
from jax import lax
from jax.experimental import pallas as pl
from jax.experimental.pallas import tpu as pltpu
from jax.sharding import PartitionSpec as P

CH = 128
NP = 100
EPS = 1e-05
CAP = 8.0
F32 = jnp.float32
BF16 = jnp.bfloat16
MESH = pl.DeviceIdType.MESH


def nn(a, b):
    return lax.dot_general(a, b, (((1,), (0,)), ((), ())), preferred_element_type=F32)


def nt(a, b):
    return lax.dot_general(a, b, (((1,), (1,)), ((), ())), preferred_element_type=F32)


def iota(shape, dim):
    return lax.broadcasted_iota(jnp.int32, shape, dim)


def split2(v):
    high = v.astype(BF16)
    return high, (v - high.astype(F32)).astype(BF16)


def split3(v):
    high = v.astype(BF16)
    rest = v - high.astype(F32)
    mid = rest.astype(BF16)
    return high, mid, (rest - mid.astype(F32)).astype(BF16)


def column(row):
    n = row.shape[1]
    return jnp.sum(jnp.where(iota((n, n), 0) == iota((n, n), 1), row, 0.0), axis=1, keepdims=True)


def convolve(current, before, taps):
    padded = jnp.concatenate([before, current], axis=0)
    total = jnp.zeros(current.shape, F32)
    for tap in range(4):
        shifted = padded if tap == 3 else pltpu.roll(padded, 3 - tap, 0)
        total = total + shifted[16:] * taps[tap : tap + 1]
    return (total / (1.0 + jnp.exp(-total))).astype(BF16)


def kernel(
    ns,
    nh,
    x,
    z,
    bc,
    dt,
    bias,
    alog,
    convx,
    convbc,
    skip,
    gain,
    weight,
    pid,
    tlogits,
    torder,
    mixed,
    tgrad,
    kl,
    xc,
    bcc,
    bt,
    tok,
    tokb,
    carries,
    lg,
    eg,
    read,
    member,
    prow,
    tail_x,
    tail_bc,
    info,
    info_all,
    s_send,
    p1,
    e_send,
    p2,
    h_send,
    h_all,
    q_send,
    q_all,
    tail_sem,
    sems,
):
    me = lax.axis_index("seq")
    mh = lax.axis_index("head")

    def seq_peer(d):
        return lax.rem(me + d, ns)

    def head_peer(d):
        return lax.rem(mh + d, nh)

    barrier = pltpu.get_barrier_semaphore()

    @pl.loop(1, ns)
    def _(d):
        pl.semaphore_signal(barrier, inc=1, device_id={"seq": seq_peer(d)}, device_id_type=MESH)

    @pl.loop(1, nh)
    def _(d):
        pl.semaphore_signal(barrier, inc=1, device_id={"head": head_peer(d)}, device_id_type=MESH)

    steps = jax.nn.softplus(dt[...] + column(bias[...]))
    rates = -jnp.exp(column(alog[...])) * steps
    upto = (iota((CH, CH), 0) <= iota((CH, CH), 1)).astype(BF16)
    stacked = jnp.concatenate([rates[:, b * CH : (b + 1) * CH] for b in range(4)], axis=0)
    cumul = sum(nn(part, upto) for part in reversed(split3(stacked)))
    pieces = []
    for b in range(4):
        here = cumul[16 * b : 16 * b + 16]
        closing = here[:, CH - 1 :]
        f1 = split2(jnp.exp(closing - here) * steps[:, b * CH : (b + 1) * CH])
        f2 = split2(jnp.exp(here))
        rows = [f1[0].astype(F32), f1[1].astype(F32), f2[0].astype(F32), f2[1].astype(F32), here]
        pieces.append(jnp.concatenate(rows + [jnp.zeros((48, CH), F32)], axis=0))
    for b in range(4):
        turned = jnp.transpose(pieces[b])
        tok[b * CH : (b + 1) * CH] = turned
        tokb[b * CH : (b + 1) * CH] = turned.astype(BF16)
    logs = sum(tok[b * CH + CH - 1 : (b + 1) * CH] for b in range(4))

    member[...] = (iota((CH, 4 * CH), 0) == pid[...]).astype(F32).astype(BF16)
    info[0:1] = nt(jnp.ones((8, 4 * CH), BF16), member[...])[0:1]
    info[1:2] = logs
    info_all[me] = info[...]

    pl.semaphore_wait(barrier, ns - 1 + nh - 1)
    right = {"seq": seq_peer(1)}
    tails = [
        pltpu.make_async_remote_copy(
            src_ref=source.at[pl.ds(4 * CH - 16, 16)],
            dst_ref=target,
            send_sem=tail_sem.at[2 * i],
            recv_sem=tail_sem.at[2 * i + 1],
            device_id=right,
            device_id_type=MESH,
        )
        for i, (source, target) in enumerate(((x, tail_x), (bc, tail_bc)))
    ]
    for copy in tails:
        copy.start()

    def seq_copy(source, target, phase, peer):
        return pltpu.make_async_remote_copy(
            src_ref=source,
            dst_ref=target,
            send_sem=sems.at[2 * phase],
            recv_sem=sems.at[2 * phase + 1],
            device_id={"seq": peer},
            device_id_type=MESH,
        )

    def head_copy(source, target, phase, peer):
        return pltpu.make_async_remote_copy(
            src_ref=source,
            dst_ref=target,
            send_sem=sems.at[2 * phase],
            recv_sem=sems.at[2 * phase + 1],
            device_id={"head": peer},
            device_id_type=MESH,
        )

    @pl.loop(1, ns)
    def _(d):
        seq_copy(info, info_all.at[me], 0, seq_peer(d)).start()

    def conv_x(b, hp, before):
        lanes = pl.ds(pl.multiple_of(hp * CH, CH), CH)
        xc[b * CH : (b + 1) * CH, lanes] = convolve(
            x[b * CH : (b + 1) * CH, lanes].astype(F32), before, convx[:, lanes].astype(F32)
        )

    def conv_bc(b, before):
        made = convolve(bc[b * CH : (b + 1) * CH].astype(F32), before, convbc[...].astype(F32))
        bcc[b * CH : (b + 1) * CH] = made
        bt[:, b * CH : (b + 1) * CH] = jnp.transpose(made[:, :CH].astype(F32)).astype(BF16)

    for b in range(1, 4):
        conv_bc(b, bc[b * CH - 16 : b * CH].astype(F32))

    @pl.loop(0, 8)
    def _(hp):
        lanes = pl.ds(pl.multiple_of(hp * CH, CH), CH)
        for b in range(1, 4):
            conv_x(b, hp, x[b * CH - 16 : b * CH, lanes].astype(F32))

    for copy in tails:
        copy.wait()
    conv_bc(0, jnp.where(me > 0, tail_bc[...].astype(F32), 0.0))

    @pl.loop(0, 8)
    def _(hp):
        lanes = pl.ds(pl.multiple_of(hp * CH, CH), CH)
        conv_x(0, hp, jnp.where(me > 0, tail_x[:, lanes].astype(F32), 0.0))
        head_of = 2 * hp + iota((CH, CH), 1) // 64
        row = iota((CH, CH), 0)
        spread1 = ((row < 32) & (row % 16 == head_of)).astype(F32).astype(BF16)
        spread2 = ((row >= 32) & (row < 64) & (row % 16 == head_of)).astype(F32).astype(BF16)
        state = None
        ahead = jnp.ones((1, CH), F32)
        for b in range(4):
            at = slice(b * CH, (b + 1) * CH)
            factor = nn(tokb[at], spread1)
            decay = nn(tokb[at], spread2)
            loaded = (xc[at, lanes].astype(F32) * factor).astype(BF16)
            added = nn(bt[:, at], loaded)
            lg[at, lanes] = decay
            eg[at, lanes] = decay * ahead
            ahead = ahead * decay[CH - 1 :]
            if b:
                carries[b - 1, 0, :, lanes], carries[b - 1, 1, :, lanes] = split2(state)
            state = added if state is None else decay[CH - 1 :] * state + added
        state = state.astype(BF16)
        for a in range(4):
            s_send[hp * 4 + a] = state[32 * a : 32 * a + 32]

    @pl.loop(1, ns)
    def _(d):
        peer = seq_peer(d)
        seq_copy(s_send.at[peer], p1.at[me], 1, peer).start()

    p1[me] = s_send[me]

    def wait_all(phase, count, source, target):
        copy = seq_copy(source.at[pl.ds(0, count)], target.at[pl.ds(0, count)], phase, seq_peer(1))
        copy.wait_recv()

    def wait_sent(phase, count, source):
        copy = seq_copy(source.at[pl.ds(0, count)], source.at[pl.ds(0, count)], phase, seq_peer(1))
        copy.wait_send()

    def inside(hp):
        lanes = pl.ds(pl.multiple_of(hp * CH, CH), CH)
        lane = iota((CH, CH), 1)
        lower = iota((CH, CH), 0) >= lane
        first = lane < 64
        skips = jnp.sum(
            jnp.where(iota((1, CH), 1) // 64 + 2 * hp == iota((16, 1), 0), column(skip[...]), 0.0),
            axis=0,
            keepdims=True,
        )
        for b in range(4):
            at = slice(b * CH, (b + 1) * CH)
            pairs = jnp.where(lower, nn(bcc[at, CH:], bt[:, at]), 0.0)
            values = xc[at, lanes]
            halves = []
            for i in range(2):
                pick = iota((CH, CH), 1) == 64 + 2 * hp + i
                later = jnp.sum(jnp.where(pick, tok[at], 0.0), axis=1, keepdims=True)
                earlier = prow[0, 2 * hp + i, :, at]
                step = prow[1, 2 * hp + i, :, at]
                halves.append((pairs * jnp.exp(jnp.minimum(later - earlier, 0.0)) * step).astype(BF16))
            blocks = jnp.concatenate(
                [jnp.where(first, values, jnp.zeros_like(values)), jnp.where(first, jnp.zeros_like(values), values)],
                axis=0,
            )
            total = nn(jnp.concatenate(halves, axis=1), blocks) + skips * values.astype(F32)
            if b:
                outer = nn(bcc[at, CH:], carries[b - 1, 0, :, lanes]) + nn(bcc[at, CH:], carries[b - 1, 1, :, lanes])
                total = total + lg[at, lanes] * outer
            gate = z[at, lanes].astype(F32)
            gate = gate * (0.5 * jnp.tanh(0.5 * gate) + 0.5)
            lg[at, lanes] = total * gate
            eg[at, lanes] = eg[at, lanes] * gate

    for h in range(16):
        for b in range(4):
            prow[0, h, :, b * CH : (b + 1) * CH] = cumul[16 * b + h : 16 * b + h + 1]
        prow[1, h] = steps[h : h + 1]

    @pl.loop(0, 4)
    def _(hp):
        inside(hp)

    wait_all(0, ns - 1, info_all, info_all)
    lane = iota((1, CH), 1)
    kept = (lane >= 64) & (lane < 80)
    decays = jnp.where(kept, jnp.exp(jnp.where(kept, info_all[:, 1, :], 0.0)), 0.0)
    spread = (iota((CH, CH), 0) == 64 + 2 * (me // 4) + iota((CH, CH), 1) // 64).astype(F32).astype(BF16)
    decays = sum(nn(part, spread) for part in reversed(split3(decays)))
    counts = jnp.sum(info_all[:, 0, :], axis=0, keepdims=True)
    wait_all(1, ns - 1, p1, p1)
    entering = jnp.zeros((32, CH), F32)
    for j in range(ns):
        e_send[j] = entering.astype(BF16)
        if j < ns - 1:
            entering = decays[j : j + 1] * entering + p1[j].astype(F32)

    @pl.loop(1, ns)
    def _(d):
        peer = seq_peer(d)
        seq_copy(e_send.at[peer], p2.at[me], 2, peer).start()

    p2[me] = e_send[me]

    @pl.loop(4, 8)
    def _(hp):
        inside(hp)

    valid = lane < NP
    ranks = jnp.where(iota((NP, NP), 0) == torder[...], tlogits[...], 0.0)
    ranks = jnp.sum(ranks, axis=1, keepdims=True)
    teacher = jnp.sum(jnp.where(iota((NP, CH), 0) == iota((NP, CH), 1), ranks, 0.0), axis=0, keepdims=True)
    teacher = teacher - jnp.log(jnp.sum(jnp.where(valid, jnp.exp(teacher), 0.0), axis=1, keepdims=True))
    share = jnp.where(valid, jnp.exp(teacher), 0.0)
    weights = jnp.broadcast_to(weight[...].astype(F32), (16, 8 * CH)).astype(BF16)
    gains = gain[...].astype(F32)

    wait_all(2, ns - 1, p2, p2)

    @pl.loop(0, 4)
    def _(b):
        at = pl.ds(pl.multiple_of(b * CH, CH), CH)
        cmat = bcc[at, CH:]
        squares = jnp.zeros((CH, CH), F32)
        for hp in range(8):
            lanes = slice(hp * CH, (hp + 1) * CH)
            state = p2[4 * hp : 4 * hp + 4].reshape(CH, CH)
            gated = lg[at, lanes] + eg[at, lanes] * nn(cmat, state)
            lg[at, lanes] = gated
            squares = squares + gated * gated
        scale = lax.rsqrt(jnp.sum(squares, axis=1, keepdims=True) / (8 * CH) + EPS)
        for hp in range(8):
            lanes = slice(hp * CH, (hp + 1) * CH)
            mixed[at, lanes] = (lg[at, lanes] * scale * gains[:, lanes]).astype(BF16)
        read[b] = nt(weights, mixed[at, :])[0:8]

    readout = jnp.concatenate([read[b] for b in range(4)], axis=1)
    part = sum(nt(part, member[...]) for part in reversed(split3(readout)))
    h_send[...] = part[0:1]
    h_all[mh] = part[0:1]

    @pl.loop(1, nh)
    def _(d):
        head_copy(h_send, h_all.at[mh], 3, head_peer(d)).start()

    wait_all(3, nh - 1, h_all, h_all)
    total = jnp.sum(h_all[...], axis=0)
    q_send[...] = total
    q_all[me] = total

    @pl.loop(1, ns)
    def _(d):
        seq_copy(q_send, q_all.at[me], 4, seq_peer(d)).start()

    wait_all(4, ns - 1, q_all, q_all)
    sums = jnp.sum(q_all[...], axis=0)
    counts = jnp.where(valid, counts, 1.0)
    squash = jnp.tanh(sums / counts / CAP)
    scores = CAP * squash
    student = scores - jnp.log(jnp.sum(jnp.where(valid, jnp.exp(scores), 0.0), axis=1, keepdims=True))
    kl[...] = jnp.sum(share * (teacher - student), axis=1, keepdims=True)
    coef = (jnp.exp(student) - share) * (1.0 - squash * squash) * (4.0 * CH * ns) / counts
    coef = jnp.broadcast_to(jnp.where(valid, coef, 0.0), (8, CH))
    tgrad[...] = sum(nn(part, member[...]) for part in reversed(split3(coef)))[0:1]

    wait_sent(0, ns - 1, info_all)
    wait_sent(1, ns - 1, s_send)
    wait_sent(2, ns - 1, e_send)
    wait_sent(3, nh - 1, h_all)
    wait_sent(4, ns - 1, q_all)


def solution(mesh):
    ns, nh = mesh.shape["seq"], mesh.shape["head"]

    def per_device(
        x_in, z_in, bc_in, dt_raw, dt_bias, a_log, conv_x, conv_bc, skip_gain, norm_gain, score_weight, passage_ids,
        teacher_logits, teacher_order,
    ):
        vmem = pl.BlockSpec(memory_space=pltpu.VMEM)
        tokens, width = x_in.shape
        mixed, tgrad, kl = pl.pallas_call(
            functools.partial(kernel, ns, nh),
            out_shape=(
                jax.ShapeDtypeStruct((tokens, width), BF16),
                jax.ShapeDtypeStruct((1, tokens), F32),
                jax.ShapeDtypeStruct((1, 1), F32),
            ),
            in_specs=[vmem] * 14,
            out_specs=(vmem, vmem, vmem),
            scratch_shapes=[
                pltpu.VMEM((tokens, width), BF16),
                pltpu.VMEM((tokens, 2 * CH), BF16),
                pltpu.VMEM((CH, tokens), BF16),
                pltpu.VMEM((tokens, CH), F32),
                pltpu.VMEM((tokens, CH), BF16),
                pltpu.VMEM((3, 2, CH, width), BF16),
                pltpu.VMEM((tokens, width), F32),
                pltpu.VMEM((tokens, width), F32),
                pltpu.VMEM((4, 8, CH), F32),
                pltpu.VMEM((CH, tokens), BF16),
                pltpu.VMEM((2, 16, 1, tokens), F32),
                pltpu.VMEM((16, width), BF16),
                pltpu.VMEM((16, 2 * CH), BF16),
                pltpu.VMEM((2, CH), F32),
                pltpu.VMEM((ns, 2, CH), F32),
                pltpu.VMEM((ns, 32, CH), BF16),
                pltpu.VMEM((ns, 32, CH), BF16),
                pltpu.VMEM((ns, 32, CH), BF16),
                pltpu.VMEM((ns, 32, CH), BF16),
                pltpu.VMEM((1, CH), F32),
                pltpu.VMEM((nh, 1, CH), F32),
                pltpu.VMEM((1, CH), F32),
                pltpu.VMEM((ns, 1, CH), F32),
                pltpu.SemaphoreType.DMA((4,)),
                pltpu.SemaphoreType.DMA((10,)),
            ],
            compiler_params=pltpu.CompilerParams(
                collective_id=0, has_side_effects=True, vmem_limit_bytes=48 * 2**20
            ),
        )(
            x_in,
            z_in,
            bc_in.reshape(tokens, 2 * CH),
            dt_raw.T,
            dt_bias[None],
            a_log[None],
            conv_x,
            conv_bc.reshape(4, 2 * CH),
            skip_gain[None],
            norm_gain[None],
            score_weight[None],
            passage_ids[None],
            teacher_logits[None],
            teacher_order[None],
        )
        return mixed, tgrad.reshape(tokens), kl.reshape(())

    return jax.shard_map(
        per_device,
        mesh=mesh,
        in_specs=(
            P("seq", "head"), P("seq", "head"), P("seq", "head", None, None), P("seq", "head"), P("head"), P("head"),
            P(None, "head"), P(None, "head", None, None), P("head"), P("head"), P("head"), P("seq"), P(), P(),
        ),
        out_specs=(P("seq", "head"), P("seq"), P()),
        check_vma=False,
    )
```

time: 356 us -> 58.3 us (0.16)
  the two profiles are of different devices: /device:TPU:32 before, /device:TPU:1 now
where the time goes in v1:
time: 58.3 us; the launch traced here: 58 us
  Pallas kernels  47.8 us (82%)
  local copies, waits for them, and re-layouts  7.7 us (13%)
  between operations  2.44 us (4%)
    pallas_call x1, Pallas kernels, per_device(): pl.pallas_call(functools.partial(kernel, ns, nh), out_shape=(jax.ShapeDty...  47.8 us
    unnamed x30, local copies, waits for them, and re-layouts  7.69 us

profile of v1, /device:TPU:1, one launch (start us, length us, event | category | flops | bytes accessed | tf_op | source)
XLA Modules:
  0.0 58.0 jit_solution(7829619550220503879)
XLA Ops:
  0.6 0.0 copy-start.12
  0.6 0.7 %copy-done.12 = bf16[4,1,2,128]{3,2,1,0:T(2,128)(2,1)S(1)} copy-done((bf16[4,1,2,128]{3,2,1,0:T(2,128)(2,1)S(1)}, bf16[4,1,2,128]{3,2,1,0:T(2,128)(2,1)}, u32[]{:S(2)}) %copy-start.12) | copy-done | bytes 2072
  1.3 0.0 copy-start.10
  1.3 0.7 %copy-done.10 = bf16[1024]{0:T(1024)(128)(2,1)S(1)} copy-done((bf16[1024]{0:T(1024)(128)(2,1)S(1)}, bf16[1024]{0:T(1024)(128)(2,1)}, u32[]{:S(2)}) %copy-start.10) | copy-done | bytes 2072
  2.0 0.0 copy-start.11
  2.0 0.7 %copy-done.11 = bf16[1024]{0:T(1024)(128)(2,1)S(1)} copy-done((bf16[1024]{0:T(1024)(128)(2,1)S(1)}, bf16[1024]{0:T(1024)(128)(2,1)}, u32[]{:S(2)}) %copy-start.11) | copy-done | bytes 2072
  2.7 0.0 copy-start.2
  2.7 0.0 copy-start.3
  2.7 0.0 copy-start.4
  2.7 0.0 copy-start.8
  2.7 0.0 copy-start.9
  2.7 1.0 %copy.21 = bf16[64,8,2,128]{3,1,2,0:T(8,128)(2,1)S(1)} copy(bf16[64,8,2,128]{3,2,1,0:T(2,128)(2,1)} %bitcast.29) | data formatting | bytes 524288
  3.7 0.0 copy-start.5
  3.8 0.0 copy-start.6
  3.8 0.0 copy-start.7
  3.8 0.0 copy-done.2
  3.8 0.0 copy-done.3
  3.8 0.0 copy-done.4
  3.8 0.0 copy-done.8
  3.8 0.0 copy-done.9
  3.8 0.6 copy-done.5
  4.4 0.0 copy-done.6
  4.4 0.0 copy-done.7
  4.4 0.0 copy-start
  4.4 1.2 %copy-done = bf16[512,1024]{1,0:T(8,128)(2,1)S(1)} copy-done((bf16[512,1024]{1,0:T(8,128)(2,1)S(1)}, bf16[512,1024]{1,0:T(8,128)(2,1)}, u32[]{:S(2)}) %copy-start) | copy-done | bytes 1048600
  5.7 0.0 copy-start.1
  5.7 1.2 %copy-done.1 = bf16[512,1024]{1,0:T(8,128)(2,1)S(1)} copy-done((bf16[512,1024]{1,0:T(8,128)(2,1)S(1)}, bf16[512,1024]{1,0:T(8,128)(2,1)}, u32[]{:S(2)}) %copy-start.1) | copy-done | bytes 1048600
  6.9 47.8 %shard_map.157 = (bf16[512,1024]{1,0:T(8,128)(2,1)S(1)}, f32[1,512]{1,0:T(1,128)S(1)}, f32[1,1]{1,0:T(1,128)}) custom-call(bf16[512,1024]{1,0:T(8,128)(2,1)S(1)} %copy-done, bf16[512,1024]{1,0:T(8,128)(2,1)S(1)} %copy-done.1, bf16[512,256]{1,0:T(8,128)(2,1)S(1)} %bitcast.19, f32[16,512]{1,0:T(8,128)S(1)} %bitcast.20, f32[1,16]{1,0:T(1,128)S(1)} %bitcast.24, ...), custom_call_target="tpu_custom_call" | custom-call | tf_op jit(solution)/shard_map/pallas_call | solution.py:392
  54.7 1.0 %copy.26 = bf16[512,1024]{1,0:T(8,128)(2,1)} copy(bf16[512,1024]{1,0:T(8,128)(2,1)S(1)} %get-tuple-element.12) | data formatting | bytes 2097152
  55.7 0.6 copy.27
  (3 shorter events, 0.0 us)
Async XLA Ops:
  0.6 0.7 %copy-start.12 = (bf16[4,1,2,128]{3,2,1,0:T(2,128)(2,1)S(1)}, bf16[4,1,2,128]{3,2,1,0:T(2,128)(2,1)}, u32[]{:S(2)}) copy-start(bf16[4,1,2,128]{3,2,1,0:T(2,128)(2,1)} %param.21) | copy-start | bytes 6148
  1.3 0.7 %copy-start.10 = (bf16[1024]{0:T(1024)(128)(2,1)S(1)}, bf16[1024]{0:T(1024)(128)(2,1)}, u32[]{:S(2)}) copy-start(bf16[1024]{0:T(1024)(128)(2,1)} %param.23) | copy-start | bytes 6148
  2.0 0.7 %copy-start.11 = (bf16[1024]{0:T(1024)(128)(2,1)S(1)}, bf16[1024]{0:T(1024)(128)(2,1)}, u32[]{:S(2)}) copy-start(bf16[1024]{0:T(1024)(128)(2,1)} %param.24) | copy-start | bytes 6148
  2.7 1.1 %copy-start.2 = (f32[512,16]{0,1:T(8,128)S(1)}, f32[512,16]{0,1:T(8,128)}, u32[]{:S(2)}) copy-start(f32[512,16]{0,1:T(8,128)} %param.17) | copy-start | bytes 98308
  2.7 1.1 %copy-start.3 = (bf16[4,1024]{1,0:T(4,128)(2,1)S(1)}, bf16[4,1024]{1,0:T(4,128)(2,1)}, u32[]{:S(2)}) copy-start(bf16[4,1024]{1,0:T(4,128)(2,1)} %convx.1) | copy-start | bytes 24580
  2.7 1.1 %copy-start.4 = (s32[512]{0:T(512)S(1)}, s32[512]{0:T(512)}, u32[]{:S(2)}) copy-start(s32[512]{0:T(512)} %param.25) | copy-start | bytes 6148
  2.7 1.1 %copy-start.8 = (f32[100]{0:T(128)S(1)}, f32[100]{0:T(128)}, u32[]{:S(2)}) copy-start(f32[100]{0:T(128)} %param.26) | copy-start | bytes 1204
  2.7 1.1 %copy-start.9 = (s32[100]{0:T(128)S(1)}, s32[100]{0:T(128)}, u32[]{:S(2)}) copy-start(s32[100]{0:T(128)} %param.27) | copy-start | bytes 1204
  3.7 0.7 %copy-start.5 = (f32[16]{0:T(128)S(1)}, f32[16]{0:T(128)}, u32[]{:S(2)}) copy-start(f32[16]{0:T(128)} %param.18) | copy-start | bytes 196
  3.8 0.7 %copy-start.6 = (f32[16]{0:T(128)S(1)}, f32[16]{0:T(128)}, u32[]{:S(2)}) copy-start(f32[16]{0:T(128)} %param.19) | copy-start | bytes 196
  3.8 0.7 %copy-start.7 = (f32[16]{0:T(128)S(1)}, f32[16]{0:T(128)}, u32[]{:S(2)}) copy-start(f32[16]{0:T(128)} %param.22) | copy-start | bytes 196
  4.4 1.2 %copy-start = (bf16[512,1024]{1,0:T(8,128)(2,1)S(1)}, bf16[512,1024]{1,0:T(8,128)(2,1)}, u32[]{:S(2)}) copy-start(bf16[512,1024]{1,0:T(8,128)(2,1)} %x.1) | copy-start | bytes 3145732
  5.7 1.2 %copy-start.1 = (bf16[512,1024]{1,0:T(8,128)(2,1)S(1)}, bf16[512,1024]{1,0:T(8,128)(2,1)}, u32[]{:S(2)}) copy-start(bf16[512,1024]{1,0:T(8,128)(2,1)} %z.1) | copy-start | bytes 3145732

commit v2 on v1

v2 whole, which is shorter than its diff:
```python
import functools

import jax
import jax.numpy as jnp
from jax import lax
from jax.experimental import pallas as pl
from jax.experimental.pallas import tpu as pltpu
from jax.sharding import PartitionSpec as P

CH = 128
NP = 100
EPS = 1e-05
CAP = 8.0
F32 = jnp.float32
BF16 = jnp.bfloat16
MESH = pl.DeviceIdType.MESH


def nn(a, b):
    return lax.dot_general(a, b, (((1,), (0,)), ((), ())), preferred_element_type=F32)


def nt(a, b):
    return lax.dot_general(a, b, (((1,), (1,)), ((), ())), preferred_element_type=F32)


def iota(shape, dim):
    return lax.broadcasted_iota(jnp.int32, shape, dim)


def split2(v):
    high = v.astype(BF16)
    return high, (v - high.astype(F32)).astype(BF16)


def split3(v):
    high = v.astype(BF16)
    rest = v - high.astype(F32)
    mid = rest.astype(BF16)
    return high, mid, (rest - mid.astype(F32)).astype(BF16)


def column(row):
    n = row.shape[1]
    return jnp.sum(jnp.where(iota((n, n), 0) == iota((n, n), 1), row, 0.0), axis=1, keepdims=True)


def silu(v):
    below = 1.0 + jnp.exp(-v)
    guess = pl.reciprocal(below, approx=True)
    return v * (guess * (2.0 - below * guess))


def convolve(current, before, taps):
    padded = jnp.concatenate([before, current], axis=0)
    total = jnp.zeros(current.shape, F32)
    for tap in range(4):
        shifted = padded if tap == 3 else pltpu.roll(padded, 3 - tap, 0)
        total = total + shifted[16:] * taps[tap : tap + 1]
    return silu(total).astype(BF16)


def spread_codes(shape, sections):
    row, lane = iota(shape, 0), iota(shape, 1)
    code = jnp.full(shape, -1, jnp.int32)
    for first, last, start, width, size in sections:
        inside = (row >= first) & (row < last) & (lane >= start) & (lane < start + width)
        code = jnp.where(inside, (row & 15) - (lane - start) // size, code)
    return code


def kernel(ns, nh, *refs):
    given, (result, tgrad, kl), held = refs[:14], refs[14:17], refs[17:31]
    x, z, bc, dt, bias, alog, convx, convbc, skip, gain, weight, pid, tlogits, torder = held
    (
        xc, cm, bt, mix, paired, tokb, tokc, spreads, codes, local, lg, eg, squares, read, member, prow, tail_x, tail_bc,
        info, info_all, s_send, p1, e_send, p2, h_send, h_all, q_send, q_all, mixed,
        in_sem, out_sem, tail_sem, sems, p2_sem,
    ) = refs[31:]
    me = lax.axis_index("seq")
    mh = lax.axis_index("head")

    def far(i):
        return 4 + (2 * lax.rem(i, 2) - 1) * ((i + 1) // 2)

    def seq_pair(i):
        return lax.rem(me // 4 + far(i), 8)

    def each_seq_peer(act):
        @pl.loop(0, ns)
        def _(t):
            peer = 4 * seq_pair(t // 4) + lax.rem(t, 4)

            @pl.when(peer != me)
            def _():
                act(peer)

    def each_head_peer(act):
        @pl.loop(0, nh - 1)
        def _(t):
            act(lax.rem(mh + far(t), nh))

    barrier = pltpu.get_barrier_semaphore()
    each_seq_peer(lambda peer: pl.semaphore_signal(barrier, inc=1, device_id={"seq": peer}, device_id_type=MESH))
    each_head_peer(lambda peer: pl.semaphore_signal(barrier, inc=1, device_id={"head": peer}, device_id_type=MESH))

    loads = [
        pltpu.make_async_copy(source, target, in_sem.at[i])
        for i, (source, target) in enumerate(zip(given, held))
    ]
    for i in (3, 4, 5, 2, 7, 0, 6, 11, 1, 8, 9, 10, 12, 13):
        loads[i].start()

    codes[...] = spread_codes((CH, 4 * CH), ((0, 32, 0, CH, 64), (32, 64, CH, CH, 64), (64, 112, 2 * CH, 2 * CH, CH)))
    for hp in range(8):
        code = spread_codes((CH, CH), ((0, 32, 0, CH, 64),))
        spreads[:, hp * CH : (hp + 1) * CH] = (code == 2 * hp).astype(F32).astype(BF16)
    squares[...] = jnp.zeros(squares.shape, F32)

    for i in (3, 4, 5):
        loads[i].wait()
    steps = jax.nn.softplus(dt[...] + column(bias[...]))
    rates = -jnp.exp(column(alog[...])) * steps
    upto = (iota((CH, CH), 0) <= iota((CH, CH), 1)).astype(F32).astype(BF16)
    stacked = jnp.concatenate([rates[:, b * CH : (b + 1) * CH] for b in range(4)], axis=0)
    cumul = sum(nn(part, upto) for part in reversed(split3(stacked)))
    logs = jnp.zeros((16, 1), F32)
    for b in reversed(range(4)):
        here = cumul[16 * b : 16 * b + 16]
        logs = logs + here[:, CH - 1 :]
        parts = split2(jnp.exp(logs - here) * steps[:, b * CH : (b + 1) * CH])
        rows = [part.astype(F32) for part in parts] + [jnp.zeros((96, CH), F32)]
        tokb[b * CH : (b + 1) * CH] = jnp.transpose(jnp.concatenate(rows, axis=0)).astype(BF16)

    even = iota((8, CH), 0) % 2 == 0
    for i in (2, 7):
        loads[i].wait()
    taps = convbc[...].astype(F32)

    def conv_bc(first, count, before):
        current = bc[2 * first : 2 * (first + count)].astype(F32)
        padded = jnp.concatenate([before, current], axis=0)
        total = jnp.zeros((count // 4, 8, CH), F32)
        for tap in range(4):
            shifted = padded if tap == 3 else pltpu.roll(padded, 2 * (3 - tap), 0)
            factor = jnp.where(even, taps[2 * tap : 2 * tap + 1], taps[2 * tap + 1 : 2 * tap + 2])
            total = total + shifted[16:].reshape(count // 4, 8, CH) * factor[None]
        mix[2 * first : 2 * (first + count)] = silu(total).reshape(2 * count, CH)

    def turn_b(b):
        bt[:, b * CH : (b + 1) * CH] = jnp.transpose(mix[pl.ds(2 * b * CH, CH, stride=2)]).astype(BF16)

    for b in range(4):
        conv_bc(b * CH, CH, bc[2 * b * CH - 16 : 2 * b * CH].astype(F32) if b else jnp.zeros((16, CH), F32))
        turn_b(b)
    for i in (0, 6):
        loads[i].wait()

    def local_state(hp):
        lanes = pl.ds(pl.multiple_of(hp * CH, CH), CH)
        factors = convx[:, lanes].astype(F32)
        loaded = []
        for b in range(4):
            at = slice(b * CH, (b + 1) * CH)
            before = x[b * CH - 16 : b * CH, lanes].astype(F32) if b else jnp.zeros((16, CH), F32)
            made = convolve(x[at, lanes].astype(F32), before, factors)
            xc[at, lanes] = made
            part = made.astype(F32) * nn(tokb[at], spreads[:, lanes])
            if b == 0:
                part = jnp.where(iota((CH, CH), 0) >= 3, part, 0.0)
            loaded.append(part.astype(BF16))
        local[:, lanes] = nn(bt[...], jnp.concatenate(loaded, axis=0))

    @pl.loop(0, 4)
    def _(hp):
        local_state(hp)

    pl.semaphore_wait(barrier, ns - 1 + nh - 1)
    tails = [
        pltpu.make_async_remote_copy(
            src_ref=source.at[pl.ds(source.shape[0] - 16, 16)],
            dst_ref=target,
            send_sem=tail_sem.at[2 * i],
            recv_sem=tail_sem.at[2 * i + 1],
            device_id={"seq": lax.rem(me + 1, ns)},
            device_id_type=MESH,
        )
        for i, (source, target) in enumerate(((x, tail_x), (bc, tail_bc)))
    ]
    for copy in tails:
        copy.start()

    @pl.loop(4, 8)
    def _(hp):
        local_state(hp)

    def copy_to(axis, source, target, phase, peer, arrived=None):
        return pltpu.make_async_remote_copy(
            src_ref=source,
            dst_ref=target,
            send_sem=sems.at[2 * phase],
            recv_sem=sems.at[2 * phase + 1] if arrived is None else arrived,
            device_id={axis: peer},
            device_id_type=MESH,
        )

    def wait_all(phase, count, buffer):
        copy_to("seq", buffer.at[pl.ds(0, count)], buffer.at[pl.ds(0, count)], phase, 0).wait_recv()

    def wait_sent(phase, count, buffer):
        copy_to("seq", buffer.at[pl.ds(0, count)], buffer.at[pl.ds(0, count)], phase, 0).wait_send()

    info[...] = jnp.sum(jnp.where(iota((16, CH), 0) == iota((16, CH), 1), logs, 0.0), axis=0, keepdims=True)
    info_all[me] = info[...]

    starts = nn(tokb[0:16], spreads[...])
    for copy in tails:
        copy.wait()
    before_bc = jnp.where(me > 0, tail_bc[...].astype(F32), 0.0)
    conv_bc(0, 16, before_bc)
    first_b = jnp.concatenate([mix[pl.ds(0, 16, stride=2)], jnp.zeros((CH - 16, CH), F32)], axis=0)
    first_b = jnp.transpose(first_b).astype(BF16)[:, :16]
    made = convolve(x[0:16].astype(F32), jnp.where(me > 0, tail_x[...].astype(F32), 0.0), convx[...].astype(F32))
    xc[0:16] = made
    first_x = jnp.where(iota(starts.shape, 0) < 3, made.astype(F32) * starts, 0.0).astype(BF16)
    for hp in range(8):
        lanes = slice(hp * CH, (hp + 1) * CH)
        state = (local[:, lanes] + nn(first_b, first_x[:, lanes])).astype(BF16)
        for a in range(4):
            s_send[hp * 4 + a] = state[32 * a : 32 * a + 32]

    each_seq_peer(lambda peer: copy_to("seq", s_send.at[peer], p1.at[me], 1, peer).start())
    each_seq_peer(lambda peer: copy_to("seq", info, info_all.at[me], 0, peer).start())
    p1[me] = s_send[me]

    for i in (1, 8, 9, 10, 11, 12, 13):
        loads[i].wait()
    conv_bc(0, CH, before_bc)
    turn_b(0)
    for b in range(4):
        at = slice(b * CH, (b + 1) * CH)
        cm[at] = mix[pl.ds(2 * b * CH + 1, CH, stride=2)].astype(BF16)
        paired[b] = jnp.where(iota((CH, CH), 0) >= iota((CH, CH), 1), nn(cm[at], bt[:, at]), 0.0)
        here = cumul[16 * b : 16 * b + 16]
        parts = split2(jnp.exp(here[:, CH - 1 :] - here) * steps[:, at]) + split2(jnp.exp(here)) + split3(here)
        rows = [part.astype(F32) for part in parts] + [jnp.zeros((16, CH), F32)]
        tokc[at] = jnp.transpose(jnp.concatenate(rows, axis=0)).astype(BF16)
        for h in range(16):
            prow[0, h, :, at] = here[h : h + 1]
    for h in range(16):
        prow[1, h] = steps[h : h + 1]
    skip_column = column(skip[...])

    def inside(hp):
        lanes = pl.ds(pl.multiple_of(hp * CH, CH), CH)
        first = iota((CH, CH), 1) < 64
        spread = (codes[...] == 2 * hp).astype(F32).astype(BF16)
        mine = iota((1, CH), 1) // 64 + 2 * hp == iota((16, 1), 0)
        skips = jnp.sum(jnp.where(mine, skip_column, 0.0), axis=0, keepdims=True)
        state = None
        ahead = jnp.ones((1, CH), F32)
        for b in range(4):
            at = slice(b * CH, (b + 1) * CH)
            wide = nn(tokc[at], spread)
            factor, decay = wide[:, :CH], wide[:, CH : 2 * CH]
            pairs = paired[b]
            values = xc[at, lanes]
            halves = []
            for i in range(2):
                later = wide[:, (i + 2) * CH : (i + 3) * CH]
                earlier = prow[0, 2 * hp + i, :, at]
                step = prow[1, 2 * hp + i, :, at]
                halves.append((pairs * jnp.exp(jnp.minimum(later - earlier, 0.0)) * step).astype(BF16))
            zeros = jnp.zeros_like(values)
            blocks = jnp.concatenate([jnp.where(first, values, zeros), jnp.where(first, zeros, values)], axis=0)
            exact = values.astype(F32)
            total = nn(jnp.concatenate(halves, axis=1), blocks) + skips * exact
            if b:
                total = total + decay * sum(nn(cm[at], part) for part in reversed(split2(state)))
            gate = z[at, lanes].astype(F32)
            gate = gate * (0.5 * jnp.tanh(0.5 * gate) + 0.5)
            lg[at, lanes] = total * gate
            eg[at, lanes] = decay * ahead * gate
            if b < 3:
                added = nn(bt[:, at], (exact * factor).astype(BF16))
                state = decay[CH - 1 :] * state + added if b else added
                ahead = ahead * decay[CH - 1 :]

    @pl.loop(0, 5)
    def _(hp):
        inside(hp)

    lane = iota((1, CH), 1)
    spread = (iota((CH, CH), 0) == 2 * (me // 4) + iota((CH, CH), 1) // 64).astype(F32).astype(BF16)
    wait_all(0, ns - 1, info_all)
    decays = jnp.where(lane < 16, jnp.exp(jnp.sum(info_all[...], axis=1)), 0.0)
    decays = sum(nn(part, spread) for part in reversed(split3(decays)))
    wait_all(1, ns - 1, p1)
    entering = jnp.zeros((32, CH), F32)
    for j in range(ns):
        e_send[j] = entering.astype(BF16)
        if j < ns - 1:
            entering = decays[j : j + 1] * entering + p1[j].astype(F32)
    each_seq_peer(lambda peer: copy_to("seq", e_send.at[peer], p2.at[me], 2, peer, p2_sem.at[me]).start())
    p2[me] = e_send[me]

    @pl.loop(5, 8)
    def _(hp):
        inside(hp)

    member[...] = (iota((CH, 4 * CH), 0) == pid[...]).astype(F32).astype(BF16)
    q_send[1:2] = nt(jnp.ones((8, 4 * CH), BF16), member[...])[0:1]
    valid = lane < NP
    ranks = jnp.where(iota((NP, NP), 0) == torder[...], tlogits[...], 0.0)
    ranks = jnp.sum(ranks, axis=1, keepdims=True)
    teacher = jnp.sum(jnp.where(iota((NP, CH), 0) == iota((NP, CH), 1), ranks, 0.0), axis=0, keepdims=True)
    teacher = teacher - jnp.log(jnp.sum(jnp.where(valid, jnp.exp(teacher), 0.0), axis=1, keepdims=True))
    share = jnp.where(valid, jnp.exp(teacher), 0.0)
    weights = weight[...].astype(F32)
    weights = jnp.concatenate([weights[hp : hp + 1] for hp in range(8)], axis=1)
    weights = jnp.broadcast_to(weights, (16, 8 * CH)).astype(BF16)
    gains = gain[...].astype(F32)

    @pl.loop(0, 8)
    def _(i):
        hp = seq_pair(7 - i)
        lanes = pl.ds(pl.multiple_of(hp * CH, CH), CH)
        for a in range(4):
            peer = 4 * hp + a

            @pl.when(peer != me)
            def _():
                copy_to("seq", p2.at[peer], p2.at[peer], 2, peer, p2_sem.at[peer]).wait_recv()

        state = p2[pl.ds(4 * hp, 4)].reshape(CH, CH)
        for b in range(4):
            at = slice(b * CH, (b + 1) * CH)
            gated = lg[at, lanes] + eg[at, lanes] * nn(cm[at], state)
            lg[at, lanes] = gated
            squares[at] += gated * gated

    def store(b):
        at = pl.ds(pl.multiple_of(b * CH, CH), CH)
        return pltpu.make_async_copy(mixed.at[at], result.at[at], out_sem.at[b])

    @pl.loop(0, 4)
    def _(b):
        at = pl.ds(pl.multiple_of(b * CH, CH), CH)
        scale = lax.rsqrt(jnp.sum(squares[at], axis=1, keepdims=True) / (8 * CH) + EPS)
        for hp in range(8):
            lanes = slice(hp * CH, (hp + 1) * CH)
            mixed[at, lanes] = (lg[at, lanes] * scale * gains[hp : hp + 1]).astype(BF16)
        read[b] = nt(weights, mixed[at, :])[0:8]
        store(b).start()

    readout = jnp.concatenate([read[b] for b in range(4)], axis=1)
    part = sum(nt(part, member[...]) for part in reversed(split3(readout)))
    h_send[...] = part[0:1]
    h_all[mh] = part[0:1]
    each_head_peer(lambda peer: copy_to("head", h_send, h_all.at[mh], 3, peer).start())
    wait_all(3, nh - 1, h_all)
    q_send[0:1] = jnp.sum(h_all[...], axis=0)
    q_all[me] = q_send[...]
    each_seq_peer(lambda peer: copy_to("seq", q_send, q_all.at[me], 4, peer).start())
    for b in range(4):
        store(b).wait()
    wait_sent(0, ns - 1, info_all)
    wait_sent(1, ns - 1, s_send)
    wait_sent(2, ns - 1, e_send)
    wait_sent(3, nh - 1, h_all)
    wait_all(4, ns - 1, q_all)
    totals = jnp.sum(q_all[...], axis=0)
    counts = jnp.where(valid, totals[1:2], 1.0)
    squash = jnp.tanh(totals[0:1] / counts / CAP)
    scores = CAP * squash
    student = scores - jnp.log(jnp.sum(jnp.where(valid, jnp.exp(scores), 0.0), axis=1, keepdims=True))
    kl[...] = jnp.sum(share * (teacher - student), axis=1, keepdims=True)
    coef = (jnp.exp(student) - share) * (1.0 - squash * squash) * (4.0 * CH * ns) / counts
    coef = jnp.broadcast_to(jnp.where(valid, coef, 0.0), (8, CH))
    tgrad[...] = sum(nn(part, member[...]) for part in reversed(split3(coef)))[0:1]
    wait_sent(4, ns - 1, q_all)


def solution(mesh):
    ns, nh = mesh.shape["seq"], mesh.shape["head"]

    def per_device(
        x_in, z_in, bc_in, dt_raw, dt_bias, a_log, conv_x, conv_bc, skip_gain, norm_gain, score_weight, passage_ids,
        teacher_logits, teacher_order,
    ):
        vmem = pl.BlockSpec(memory_space=pltpu.VMEM)
        hbm = pl.BlockSpec(memory_space=pltpu.HBM)
        tokens, width = x_in.shape
        given = (
            x_in,
            z_in,
            bc_in.reshape(2 * tokens, CH),
            dt_raw.T,
            dt_bias[None],
            a_log[None],
            conv_x,
            conv_bc.reshape(8, CH),
            skip_gain[None],
            norm_gain.reshape(8, CH),
            score_weight.reshape(8, CH),
            passage_ids[None],
            teacher_logits[None],
            teacher_order[None],
        )
        mixed, tgrad, kl = pl.pallas_call(
            functools.partial(kernel, ns, nh),
            out_shape=(
                jax.ShapeDtypeStruct((tokens, width), BF16),
                jax.ShapeDtypeStruct((1, tokens), F32),
                jax.ShapeDtypeStruct((1, 1), F32),
            ),
            in_specs=[hbm] * 14,
            out_specs=(hbm, vmem, vmem),
            scratch_shapes=[
                *(pltpu.VMEM(array.shape, array.dtype) for array in given),
                pltpu.VMEM((tokens, width), BF16),
                pltpu.VMEM((tokens, CH), BF16),
                pltpu.VMEM((CH, tokens), BF16),
                pltpu.VMEM((2 * tokens, CH), F32),
                pltpu.VMEM((4, CH, CH), F32),
                pltpu.VMEM((tokens, CH), BF16),
                pltpu.VMEM((tokens, CH), BF16),
                pltpu.VMEM((CH, width), BF16),
                pltpu.VMEM((CH, 4 * CH), jnp.int32),
                pltpu.VMEM((CH, width), F32),
                pltpu.VMEM((tokens, width), F32),
                pltpu.VMEM((tokens, width), F32),
                pltpu.VMEM((tokens, CH), F32),
                pltpu.VMEM((4, 8, CH), F32),
                pltpu.VMEM((CH, tokens), BF16),
                pltpu.VMEM((2, 16, 1, tokens), F32),
                pltpu.VMEM((16, width), BF16),
                pltpu.VMEM((16, CH), BF16),
                pltpu.VMEM((1, CH), F32),
                pltpu.VMEM((ns, 1, CH), F32),
                pltpu.VMEM((ns, 32, CH), BF16),
                pltpu.VMEM((ns, 32, CH), BF16),
                pltpu.VMEM((ns, 32, CH), BF16),
                pltpu.VMEM((ns, 32, CH), BF16),
                pltpu.VMEM((1, CH), F32),
                pltpu.VMEM((nh, 1, CH), F32),
                pltpu.VMEM((2, CH), F32),
                pltpu.VMEM((ns, 2, CH), F32),
                pltpu.VMEM((tokens, width), BF16),
                pltpu.SemaphoreType.DMA((14,)),
                pltpu.SemaphoreType.DMA((4,)),
                pltpu.SemaphoreType.DMA((4,)),
                pltpu.SemaphoreType.DMA((10,)),
                pltpu.SemaphoreType.DMA((ns,)),
            ],
            compiler_params=pltpu.CompilerParams(
                collective_id=0, has_side_effects=True, vmem_limit_bytes=63_400_000
            ),
        )(*given)
        return mixed, tgrad.reshape(tokens), kl.reshape(())

    return jax.shard_map(
        per_device,
        mesh=mesh,
        in_specs=(
            P("seq", "head"), P("seq", "head"), P("seq", "head", None, None), P("seq", "head"), P("head"), P("head"),
            P(None, "head"), P(None, "head", None, None), P("head"), P("head"), P("head"), P("seq"), P(), P(),
        ),
        out_specs=(P("seq", "head"), P("seq"), P()),
        check_vma=False,
    )
```

time: 58.3 us -> 53.3 us (0.914)
  local copies, waits for them, and re-layouts: 7.7 us -> 2.85 us
    unnamed x30 -> x4, local copies, waits for them, and re-layouts: 7.69 us -> 2.85 us
where the time goes in v2:
time: 53.3 us; the launch traced here: 53.1 us
  Pallas kernels  47.9 us (90%)
  local copies, waits for them, and re-layouts  2.85 us (5%)
  between operations  2.41 us (5%)
    pallas_call x1, Pallas kernels, per_device(): pl.pallas_call(functools.partial(kernel, ns, nh), out_shape=(jax.ShapeDty...  47.9 us
    unnamed x4, local copies, waits for them, and re-layouts  2.85 us

profile of v2, /device:TPU:1, one launch (start us, length us, event | category | flops | bytes accessed | tf_op | source)
XLA Modules:
  0.0 53.1 jit_solution(14852883187429751562)
XLA Ops:
  0.6 47.9 %shard_map.157 = (bf16[512,1024]{1,0:T(8,128)(2,1)}, f32[1,512]{1,0:T(1,128)}, f32[1,1]{1,0:T(1,128)}) custom-call(bf16[512,1024]{1,0:T(8,128)(2,1)} %refs_0_.1, bf16[512,1024]{1,0:T(8,128)(2,1)} %refs_1_.1, bf16[1024,128]{1,0:T(8,128)(2,1)} %bitcast.13, f32[16,512]{1,0:T(8,128)} %bitcast.14, f32[1,16]{1,0:T(1,128)} %bitcast.20, f32[1,16]{1,0:T(1,128)} %bitcast.21, ...), custom_call_target="tpu_custom_call" | custom-call | tf_op jit(solution)/shard_map/pallas_call | solution.py:410
  48.5 0.0 copy-start
  48.5 2.3 %copy.20 = bf16[512,1024]{1,0:T(8,128)(2,1)} copy(bf16[512,1024]{1,0:T(8,128)(2,1)} %get-tuple-element.12) | data formatting | bytes 2097152
  50.8 0.0 copy-done
  50.8 0.6 %copy.21 = f32[512]{0:T(512)} copy(f32[512]{0:T(512)S(1)} %bitcast.19) | data formatting | bytes 4096
Async XLA Ops:
  48.5 2.3 %copy-start = (f32[1,512]{1,0:T(1,128)S(1)}, f32[1,512]{1,0:T(1,128)}, u32[]{:S(2)}) copy-start(f32[1,512]{1,0:T(1,128)} %get-tuple-element.7) | copy-start | bytes 6148

commit v3 on v2

--- a/solution.py
+++ b/solution.py
@@ -14,6 +14,9 @@
 F32 = jnp.float32
 BF16 = jnp.bfloat16
 MESH = pl.DeviceIdType.MESH
+FAR = (4, 5, 3, 6, 2, 7, 1, 0)
+PARTS = 1
+PART = 32 // PARTS
 
 
 def nn(a, b):
@@ -70,12 +73,12 @@
 
 
 def kernel(ns, nh, *refs):
-    given, (result, tgrad, kl), held = refs[:14], refs[14:17], refs[17:31]
+    given, (mixed, tgrad, kl), held = refs[:14], refs[14:17], refs[17:31]
     x, z, bc, dt, bias, alog, convx, convbc, skip, gain, weight, pid, tlogits, torder = held
     (
         xc, cm, bt, mix, paired, tokb, tokc, spreads, codes, local, lg, eg, squares, read, member, prow, tail_x, tail_bc,
-        info, info_all, s_send, p1, e_send, p2, h_send, h_all, q_send, q_all, mixed,
-        in_sem, out_sem, tail_sem, sems, p2_sem,
+        info, info_all, s_send, p1, e_send, p2, h_send, h_all, q_send, q_all,
+        in_sem, tail_sem, sems, p2_sem,
     ) = refs[31:]
     me = lax.axis_index("seq")
     mh = lax.axis_index("head")
@@ -87,18 +90,17 @@
         return lax.rem(me // 4 + far(i), 8)
 
     def each_seq_peer(act):
-        @pl.loop(0, ns)
-        def _(t):
-            peer = 4 * seq_pair(t // 4) + lax.rem(t, 4)
-
-            @pl.when(peer != me)
-            def _():
-                act(peer)
+        for offset in FAR:
+            pair = lax.rem(me // 4 + offset, 8)
+            for a in range(4):
+                if offset:
+                    act(4 * pair + a)
+                else:
+                    pl.when(4 * pair + a != me)(functools.partial(act, 4 * pair + a))
 
     def each_head_peer(act):
-        @pl.loop(0, nh - 1)
-        def _(t):
-            act(lax.rem(mh + far(t), nh))
+        for offset in FAR[: nh - 1]:
+            act(lax.rem(mh + offset, nh))
 
     barrier = pltpu.get_barrier_semaphore()
     each_seq_peer(lambda peer: pl.semaphore_signal(barrier, inc=1, device_id={"seq": peer}, device_id_type=MESH))
@@ -227,11 +229,17 @@
         lanes = slice(hp * CH, (hp + 1) * CH)
         state = (local[:, lanes] + nn(first_b, first_x[:, lanes])).astype(BF16)
         for a in range(4):
-            s_send[hp * 4 + a] = state[32 * a : 32 * a + 32]
-
-    each_seq_peer(lambda peer: copy_to("seq", s_send.at[peer], p1.at[me], 1, peer).start())
+            for q in range(PARTS):
+                s_send[q, hp * 4 + a] = state[32 * a + PART * q : 32 * a + PART * (q + 1)]
+
+    def send_states(q):
+        each_seq_peer(lambda peer: copy_to("seq", s_send.at[q, peer], p1.at[q, me], 3 + q, peer).start())
+        p1[q, me] = s_send[q, me]
+
+    send_states(0)
     each_seq_peer(lambda peer: copy_to("seq", info, info_all.at[me], 0, peer).start())
-    p1[me] = s_send[me]
+    for q in range(1, PARTS):
+        send_states(q)
 
     for i in (1, 8, 9, 10, 11, 12, 13):
         loads[i].wait()
@@ -295,14 +303,23 @@
     wait_all(0, ns - 1, info_all)
     decays = jnp.where(lane < 16, jnp.exp(jnp.sum(info_all[...], axis=1)), 0.0)
     decays = sum(nn(part, spread) for part in reversed(split3(decays)))
-    wait_all(1, ns - 1, p1)
-    entering = jnp.zeros((32, CH), F32)
-    for j in range(ns):
-        e_send[j] = entering.astype(BF16)
-        if j < ns - 1:
-            entering = decays[j : j + 1] * entering + p1[j].astype(F32)
-    each_seq_peer(lambda peer: copy_to("seq", e_send.at[peer], p2.at[me], 2, peer, p2_sem.at[me]).start())
-    p2[me] = e_send[me]
+
+    def send_entering(q):
+        def act(peer):
+            arrived = p2_sem.at[q, me]
+            copy_to("seq", e_send.at[q, peer], p2.at[me, pl.ds(PART * q, PART)], 3 + PARTS + q, peer, arrived).start()
+
+        wait_all(3 + q, ns - 1, p1.at[q])
+        entering = jnp.zeros((PART, CH), F32)
+        for j in range(ns):
+            e_send[q, j] = entering.astype(BF16)
+            if j < ns - 1:
+                entering = decays[j : j + 1] * entering + p1[q, j].astype(F32)
+        each_seq_peer(act)
+        p2[me, PART * q : PART * (q + 1)] = e_send[q, me]
+
+    for q in range(PARTS):
+        send_entering(q)
 
     @pl.loop(5, 8)
     def _(hp):
@@ -317,20 +334,20 @@
     teacher = teacher - jnp.log(jnp.sum(jnp.where(valid, jnp.exp(teacher), 0.0), axis=1, keepdims=True))
     share = jnp.where(valid, jnp.exp(teacher), 0.0)
     weights = weight[...].astype(F32)
-    weights = jnp.concatenate([weights[hp : hp + 1] for hp in range(8)], axis=1)
-    weights = jnp.broadcast_to(weights, (16, 8 * CH)).astype(BF16)
     gains = gain[...].astype(F32)
 
     @pl.loop(0, 8)
     def _(i):
-        hp = seq_pair(7 - i)
+        hp = seq_pair(i)
         lanes = pl.ds(pl.multiple_of(hp * CH, CH), CH)
         for a in range(4):
             peer = 4 * hp + a
 
             @pl.when(peer != me)
             def _():
-                copy_to("seq", p2.at[peer], p2.at[peer], 2, peer, p2_sem.at[peer]).wait_recv()
+                for q in range(PARTS):
+                    piece = p2.at[peer, pl.ds(PART * q, PART)]
+                    copy_to("seq", piece, piece, 0, peer, p2_sem.at[q, peer]).wait_recv()
 
         state = p2[pl.ds(4 * hp, 4)].reshape(CH, CH)
         for b in range(4):
@@ -339,36 +356,33 @@
             lg[at, lanes] = gated
             squares[at] += gated * gated
 
-    def store(b):
-        at = pl.ds(pl.multiple_of(b * CH, CH), CH)
-        return pltpu.make_async_copy(mixed.at[at], result.at[at], out_sem.at[b])
-
-    @pl.loop(0, 4)
-    def _(b):
-        at = pl.ds(pl.multiple_of(b * CH, CH), CH)
+    ones = jnp.ones((16, CH), BF16)
+    for b in range(4):
+        at = slice(b * CH, (b + 1) * CH)
         scale = lax.rsqrt(jnp.sum(squares[at], axis=1, keepdims=True) / (8 * CH) + EPS)
         for hp in range(8):
             lanes = slice(hp * CH, (hp + 1) * CH)
-            mixed[at, lanes] = (lg[at, lanes] * scale * gains[hp : hp + 1]).astype(BF16)
-        read[b] = nt(weights, mixed[at, :])[0:8]
-        store(b).start()
+            made = (lg[at, lanes] * scale * gains[hp : hp + 1]).astype(BF16)
+            mixed[at, lanes] = made
+            term = made.astype(F32) * weights[hp : hp + 1]
+            total = total + term if hp else term
+        read[b] = sum(nt(ones, part) for part in reversed(split3(total)))[0:8]
 
     readout = jnp.concatenate([read[b] for b in range(4)], axis=1)
     part = sum(nt(part, member[...]) for part in reversed(split3(readout)))
     h_send[...] = part[0:1]
     h_all[mh] = part[0:1]
-    each_head_peer(lambda peer: copy_to("head", h_send, h_all.at[mh], 3, peer).start())
-    wait_all(3, nh - 1, h_all)
+    each_head_peer(lambda peer: copy_to("head", h_send, h_all.at[mh], 1, peer).start())
+    wait_all(1, nh - 1, h_all)
     q_send[0:1] = jnp.sum(h_all[...], axis=0)
     q_all[me] = q_send[...]
-    each_seq_peer(lambda peer: copy_to("seq", q_send, q_all.at[me], 4, peer).start())
-    for b in range(4):
-        store(b).wait()
+    each_seq_peer(lambda peer: copy_to("seq", q_send, q_all.at[me], 2, peer).start())
     wait_sent(0, ns - 1, info_all)
-    wait_sent(1, ns - 1, s_send)
-    wait_sent(2, ns - 1, e_send)
-    wait_sent(3, nh - 1, h_all)
-    wait_all(4, ns - 1, q_all)
+    for q in range(PARTS):
+        wait_sent(3 + q, ns - 1, s_send.at[q])
+        wait_sent(3 + PARTS + q, ns - 1, e_send.at[q])
+    wait_sent(1, nh - 1, h_all)
+    wait_all(2, ns - 1, q_all)
     totals = jnp.sum(q_all[...], axis=0)
     counts = jnp.where(valid, totals[1:2], 1.0)
     squash = jnp.tanh(totals[0:1] / counts / CAP)
@@ -378,7 +392,7 @@
     coef = (jnp.exp(student) - share) * (1.0 - squash * squash) * (4.0 * CH * ns) / counts
     coef = jnp.broadcast_to(jnp.where(valid, coef, 0.0), (8, CH))
     tgrad[...] = sum(nn(part, member[...]) for part in reversed(split3(coef)))[0:1]
-    wait_sent(4, ns - 1, q_all)
+    wait_sent(2, ns - 1, q_all)
 
 
 def solution(mesh):
@@ -410,12 +424,12 @@
         mixed, tgrad, kl = pl.pallas_call(
             functools.partial(kernel, ns, nh),
             out_shape=(
-                jax.ShapeDtypeStruct((tokens, width), BF16),
-                jax.ShapeDtypeStruct((1, tokens), F32),
+                pltpu.VMEM((tokens, width), BF16),
+                pltpu.VMEM((1, tokens), F32),
                 jax.ShapeDtypeStruct((1, 1), F32),
             ),
             in_specs=[hbm] * 14,
-            out_specs=(hbm, vmem, vmem),
+            out_specs=(vmem, vmem, vmem),
             scratch_shapes=[
                 *(pltpu.VMEM(array.shape, array.dtype) for array in given),
                 pltpu.VMEM((tokens, width), BF16),
@@ -438,25 +452,23 @@
                 pltpu.VMEM((16, CH), BF16),
                 pltpu.VMEM((1, CH), F32),
                 pltpu.VMEM((ns, 1, CH), F32),
-                pltpu.VMEM((ns, 32, CH), BF16),
-                pltpu.VMEM((ns, 32, CH), BF16),
-                pltpu.VMEM((ns, 32, CH), BF16),
+                pltpu.VMEM((PARTS, ns, PART, CH), BF16),
+                pltpu.VMEM((PARTS, ns, PART, CH), BF16),
+                pltpu.VMEM((PARTS, ns, PART, CH), BF16),
                 pltpu.VMEM((ns, 32, CH), BF16),
                 pltpu.VMEM((1, CH), F32),
                 pltpu.VMEM((nh, 1, CH), F32),
                 pltpu.VMEM((2, CH), F32),
                 pltpu.VMEM((ns, 2, CH), F32),
-                pltpu.VMEM((tokens, width), BF16),
                 pltpu.SemaphoreType.DMA((14,)),
                 pltpu.SemaphoreType.DMA((4,)),
-                pltpu.SemaphoreType.DMA((4,)),
-                pltpu.SemaphoreType.DMA((10,)),
-                pltpu.SemaphoreType.DMA((ns,)),
+                pltpu.SemaphoreType.DMA((2 * (3 + 2 * PARTS),)),
+                pltpu.SemaphoreType.DMA((PARTS, ns)),
             ],
             compiler_params=pltpu.CompilerParams(
-                collective_id=0, has_side_effects=True, vmem_limit_bytes=63_400_000
+                collective_id=0, has_side_effects=True, vmem_limit_bytes=40 * 2**20
             ),
-        )(*given)
+        )(*(pltpu.with_memory_space_constraint(array, pltpu.HBM) for array in given))
         return mixed, tgrad.reshape(tokens), kl.reshape(())
 
     return jax.shard_map(

time: 53.3 us -> 48.1 us (0.902)
  Pallas kernels: 47.9 us -> 44.1 us
  local copies, waits for them, and re-layouts: 2.85 us -> 1.55 us
    pallas_call x1, Pallas kernels: 47.9 us -> 44.1 us  [per_device(): pl.pallas_call(functools.partial(kernel, ns, nh), out_shape=(pltpu.VMEM((...]
    unnamed x4 -> x2, local copies, waits for them, and re-layouts: 2.85 us -> 1.55 us
where the time goes in v3:
time: 48.1 us; the launch traced here: 48 us
  Pallas kernels  44.1 us (92%)
  between operations  2.33 us (5%)
  local copies, waits for them, and re-layouts  1.55 us (3%)
    pallas_call x1, Pallas kernels, per_device(): pl.pallas_call(functools.partial(kernel, ns, nh), out_shape=(pltpu.VMEM((...  44.1 us
    unnamed x2, local copies, waits for them, and re-layouts  1.55 us

profile of v3, /device:TPU:1, one launch (start us, length us, event | category | flops | bytes accessed | tf_op | source)
XLA Modules:
  0.0 48.0 jit_solution(16587536690022605082)
XLA Ops:
  0.6 44.1 %shard_map.157 = (bf16[512,1024]{1,0:T(8,128)(2,1)S(1)}, f32[1,512]{1,0:T(1,128)S(1)}, f32[1,1]{1,0:T(1,128)}) custom-call(bf16[512,1024]{1,0:T(8,128)(2,1)} %refs_0_.1, bf16[512,1024]{1,0:T(8,128)(2,1)} %refs_1_.1, bf16[1024,128]{1,0:T(8,128)(2,1)} %bitcast.14, f32[16,512]{1,0:T(8,128)} %bitcast.15, f32[1,16]{1,0:T(1,128)} %bitcast.20, f32[1,16]{1,0:T(1,128)} %bitcast.21, ...), custom_call_target="tpu_custom_call" | custom-call | tf_op jit(solution)/shard_map/pallas_call | solution.py:424
  44.7 1.0 %copy.20 = bf16[512,1024]{1,0:T(8,128)(2,1)} copy(bf16[512,1024]{1,0:T(8,128)(2,1)S(1)} %get-tuple-element.9) | data formatting | bytes 2097152
  45.7 0.6 %copy.21 = f32[512]{0:T(512)} copy(f32[512]{0:T(512)S(1)} %bitcast.13) | data formatting | bytes 4096

commit v4 on v3

--- a/solution.py
+++ b/solution.py
@@ -14,7 +14,12 @@
 F32 = jnp.float32
 BF16 = jnp.bfloat16
 MESH = pl.DeviceIdType.MESH
-FAR = (4, 5, 3, 6, 2, 7, 1, 0)
+FAR = (4, 5, 3, 6, 2, 7, 1)
+NX, NZ = 4, 8
+SHIFTS = sorted(
+    ((dx, dz) for dx in range(NX) for dz in range(NZ) if dx or dz),
+    key=lambda shift: -min(shift[0], NX - shift[0]) - min(shift[1], NZ - shift[1]),
+)
 PARTS = 1
 PART = 32 // PARTS
 
@@ -76,7 +81,7 @@
     given, (mixed, tgrad, kl), held = refs[:14], refs[14:17], refs[17:31]
     x, z, bc, dt, bias, alog, convx, convbc, skip, gain, weight, pid, tlogits, torder = held
     (
-        xc, cm, bt, mix, paired, tokb, tokc, spreads, codes, local, lg, eg, squares, read, member, prow, tail_x, tail_bc,
+        xc, cm, bt, mix, paired, tokb, tokc, spreads, codes, local, lg, eg, squares, scored, both, member, prow, tail_x, tail_bc,
         info, info_all, s_send, p1, e_send, p2, h_send, h_all, q_send, q_all,
         in_sem, tail_sem, sems, p2_sem,
     ) = refs[31:]
@@ -90,16 +95,11 @@
         return lax.rem(me // 4 + far(i), 8)
 
     def each_seq_peer(act):
+        for dx, dz in SHIFTS:
+            act(lax.rem(me // NZ + dx, NX) * NZ + lax.rem(lax.rem(me, NZ) + dz, NZ))
+
+    def each_head_peer(act):
         for offset in FAR:
-            pair = lax.rem(me // 4 + offset, 8)
-            for a in range(4):
-                if offset:
-                    act(4 * pair + a)
-                else:
-                    pl.when(4 * pair + a != me)(functools.partial(act, 4 * pair + a))
-
-    def each_head_peer(act):
-        for offset in FAR[: nh - 1]:
             act(lax.rem(mh + offset, nh))
 
     barrier = pltpu.get_barrier_semaphore()
@@ -118,6 +118,7 @@
         code = spread_codes((CH, CH), ((0, 32, 0, CH, 64),))
         spreads[:, hp * CH : (hp + 1) * CH] = (code == 2 * hp).astype(F32).astype(BF16)
     squares[...] = jnp.zeros(squares.shape, F32)
+    scored[...] = jnp.zeros(scored.shape, F32)
 
     for i in (3, 4, 5):
         loads[i].wait()
@@ -214,6 +215,7 @@
 
     info[...] = jnp.sum(jnp.where(iota((16, CH), 0) == iota((16, CH), 1), logs, 0.0), axis=0, keepdims=True)
     info_all[me] = info[...]
+    each_seq_peer(lambda peer: copy_to("seq", info, info_all.at[me], 0, peer).start())
 
     starts = nn(tokb[0:16], spreads[...])
     for copy in tails:
@@ -237,7 +239,6 @@
         p1[q, me] = s_send[q, me]
 
     send_states(0)
-    each_seq_peer(lambda peer: copy_to("seq", info, info_all.at[me], 0, peer).start())
     for q in range(1, PARTS):
         send_states(q)
 
@@ -333,46 +334,54 @@
     teacher = jnp.sum(jnp.where(iota((NP, CH), 0) == iota((NP, CH), 1), ranks, 0.0), axis=0, keepdims=True)
     teacher = teacher - jnp.log(jnp.sum(jnp.where(valid, jnp.exp(teacher), 0.0), axis=1, keepdims=True))
     share = jnp.where(valid, jnp.exp(teacher), 0.0)
-    weights = weight[...].astype(F32)
     gains = gain[...].astype(F32)
-
-    @pl.loop(0, 8)
-    def _(i):
-        hp = seq_pair(i)
-        lanes = pl.ds(pl.multiple_of(hp * CH, CH), CH)
-        for a in range(4):
-            peer = 4 * hp + a
-
-            @pl.when(peer != me)
-            def _():
-                for q in range(PARTS):
-                    piece = p2.at[peer, pl.ds(PART * q, PART)]
-                    copy_to("seq", piece, piece, 0, peer, p2_sem.at[q, peer]).wait_recv()
-
-        state = p2[pl.ds(4 * hp, 4)].reshape(CH, CH)
+    products = gains * weight[...].astype(F32)
+    for hp in range(8):
+        both[hp] = products[hp : hp + 1]
+
+    @pl.loop(0, 4)
+    def _(step):
+        pairs = [seq_pair(2 * step + i) for i in range(2)]
+        for hp in pairs:
+            for a in range(4):
+                peer = 4 * hp + a
+
+                @pl.when(peer != me)
+                def _():
+                    for q in range(PARTS):
+                        piece = p2.at[peer, pl.ds(PART * q, PART)]
+                        copy_to("seq", piece, piece, 0, peer, p2_sem.at[q, peer]).wait_recv()
+
         for b in range(4):
             at = slice(b * CH, (b + 1) * CH)
-            gated = lg[at, lanes] + eg[at, lanes] * nn(cm[at], state)
-            lg[at, lanes] = gated
-            squares[at] += gated * gated
+            power, score = squares[at], scored[at]
+            for hp in pairs:
+                lanes = pl.ds(pl.multiple_of(hp * CH, CH), CH)
+                state = p2[pl.ds(4 * hp, 4)].reshape(CH, CH)
+                gated = lg[at, lanes] + eg[at, lanes] * nn(cm[at], state)
+                lg[at, lanes] = gated
+                power = power + gated * gated
+                score = score + gated * both[hp]
+            squares[at], scored[at] = power, score
 
     ones = jnp.ones((16, CH), BF16)
+    readout = []
+    for b in range(4):
+        at = slice(b * CH, (b + 1) * CH)
+        power = sum(nt(ones, part) for part in reversed(split3(squares[at])))[0:8]
+        plain = sum(nt(ones, part) for part in reversed(split3(scored[at])))[0:8]
+        readout.append(plain * lax.rsqrt(power / (8 * CH) + EPS))
+    part = sum(nt(part, member[...]) for part in reversed(split3(jnp.concatenate(readout, axis=1))))
+    h_send[...] = part[0:1]
+    h_all[mh] = part[0:1]
+    each_head_peer(lambda peer: copy_to("head", h_send, h_all.at[mh], 1, peer).start())
+
     for b in range(4):
         at = slice(b * CH, (b + 1) * CH)
         scale = lax.rsqrt(jnp.sum(squares[at], axis=1, keepdims=True) / (8 * CH) + EPS)
         for hp in range(8):
             lanes = slice(hp * CH, (hp + 1) * CH)
-            made = (lg[at, lanes] * scale * gains[hp : hp + 1]).astype(BF16)
-            mixed[at, lanes] = made
-            term = made.astype(F32) * weights[hp : hp + 1]
-            total = total + term if hp else term
-        read[b] = sum(nt(ones, part) for part in reversed(split3(total)))[0:8]
-
-    readout = jnp.concatenate([read[b] for b in range(4)], axis=1)
-    part = sum(nt(part, member[...]) for part in reversed(split3(readout)))
-    h_send[...] = part[0:1]
-    h_all[mh] = part[0:1]
-    each_head_peer(lambda peer: copy_to("head", h_send, h_all.at[mh], 1, peer).start())
+            mixed[at, lanes] = (lg[at, lanes] * scale * gains[hp : hp + 1]).astype(BF16)
     wait_all(1, nh - 1, h_all)
     q_send[0:1] = jnp.sum(h_all[...], axis=0)
     q_all[me] = q_send[...]
@@ -445,7 +454,8 @@
                 pltpu.VMEM((tokens, width), F32),
                 pltpu.VMEM((tokens, width), F32),
                 pltpu.VMEM((tokens, CH), F32),
-                pltpu.VMEM((4, 8, CH), F32),
+                pltpu.VMEM((tokens, CH), F32),
+                pltpu.VMEM((8, 1, CH), F32),
                 pltpu.VMEM((CH, tokens), BF16),
                 pltpu.VMEM((2, 16, 1, tokens), F32),
                 pltpu.VMEM((16, width), BF16),

time: 48.1 us -> 46 us (0.956)
  Pallas kernels: 44.1 us -> 42 us
    pallas_call x1, Pallas kernels: 44.1 us -> 42 us  [per_device(): pl.pallas_call(functools.partial(kernel, ns, nh), out_shape=(pltpu.VMEM((...]
where the time goes in v4:
time: 46 us; the launch traced here: 45.9 us
  Pallas kernels  42 us (91%)
  between operations  2.33 us (5%)
  local copies, waits for them, and re-layouts  1.55 us (3%)
    pallas_call x1, Pallas kernels, per_device(): pl.pallas_call(functools.partial(kernel, ns, nh), out_shape=(pltpu.VMEM((...  42 us
    unnamed x2, local copies, waits for them, and re-layouts  1.55 us

profile of v4, /device:TPU:1, one launch (start us, length us, event | category | flops | bytes accessed | tf_op | source)
XLA Modules:
  0.0 45.9 jit_solution(8805458396109430563)
XLA Ops:
  0.6 42.0 %shard_map.157 = (bf16[512,1024]{1,0:T(8,128)(2,1)S(1)}, f32[1,512]{1,0:T(1,128)S(1)}, f32[1,1]{1,0:T(1,128)}) custom-call(bf16[512,1024]{1,0:T(8,128)(2,1)} %refs_0_.1, bf16[512,1024]{1,0:T(8,128)(2,1)} %refs_1_.1, bf16[1024,128]{1,0:T(8,128)(2,1)} %bitcast.14, f32[16,512]{1,0:T(8,128)} %bitcast.15, f32[1,16]{1,0:T(1,128)} %bitcast.20, f32[1,16]{1,0:T(1,128)} %bitcast.21, ...), custom_call_target="tpu_custom_call" | custom-call | tf_op jit(solution)/shard_map/pallas_call | solution.py:433
  42.6 1.0 %copy.20 = bf16[512,1024]{1,0:T(8,128)(2,1)} copy(bf16[512,1024]{1,0:T(8,128)(2,1)S(1)} %get-tuple-element.9) | data formatting | bytes 2097152
  43.6 0.6 %copy.21 = f32[512]{0:T(512)} copy(f32[512]{0:T(512)S(1)} %bitcast.13) | data formatting | bytes 4096

commit v5 on v4

--- a/solution.py
+++ b/solution.py
@@ -174,7 +174,7 @@
             loaded.append(part.astype(BF16))
         local[:, lanes] = nn(bt[...], jnp.concatenate(loaded, axis=0))
 
-    @pl.loop(0, 4)
+    @pl.loop(0, 4, unroll=2)
     def _(hp):
         local_state(hp)
 
@@ -193,7 +193,7 @@
     for copy in tails:
         copy.start()
 
-    @pl.loop(4, 8)
+    @pl.loop(4, 8, unroll=2)
     def _(hp):
         local_state(hp)
 
@@ -339,7 +339,7 @@
     for hp in range(8):
         both[hp] = products[hp : hp + 1]
 
-    @pl.loop(0, 4)
+    @pl.loop(0, 4, unroll=2)
     def _(step):
         pairs = [seq_pair(2 * step + i) for i in range(2)]
         for hp in pairs:

time: 46 us -> 45.8 us (level)
  no operation moved by 1% of the time
where the time goes in v5:
time: 45.8 us; the launch traced here: 45.7 us
  Pallas kernels  41.8 us (91%)
  between operations  2.33 us (5%)
  local copies, waits for them, and re-layouts  1.55 us (3%)
    pallas_call x1, Pallas kernels, per_device(): pl.pallas_call(functools.partial(kernel, ns, nh), out_shape=(pltpu.VMEM((...  41.8 us
    unnamed x2, local copies, waits for them, and re-layouts  1.55 us

profile of v5, /device:TPU:1, one launch (start us, length us, event | category | flops | bytes accessed | tf_op | source)
XLA Modules:
  0.0 45.7 jit_solution(714402167345248752)
XLA Ops:
  0.6 41.8 %shard_map.157 = (bf16[512,1024]{1,0:T(8,128)(2,1)S(1)}, f32[1,512]{1,0:T(1,128)S(1)}, f32[1,1]{1,0:T(1,128)}) custom-call(bf16[512,1024]{1,0:T(8,128)(2,1)} %refs_0_.1, bf16[512,1024]{1,0:T(8,128)(2,1)} %refs_1_.1, bf16[1024,128]{1,0:T(8,128)(2,1)} %bitcast.14, f32[16,512]{1,0:T(8,128)} %bitcast.15, f32[1,16]{1,0:T(1,128)} %bitcast.20, f32[1,16]{1,0:T(1,128)} %bitcast.21, ...), custom_call_target="tpu_custom_call" | custom-call | tf_op jit(solution)/shard_map/pallas_call | solution.py:433
  42.4 1.0 %copy.20 = bf16[512,1024]{1,0:T(8,128)(2,1)} copy(bf16[512,1024]{1,0:T(8,128)(2,1)S(1)} %get-tuple-element.9) | data formatting | bytes 2097152
  43.4 0.6 %copy.21 = f32[512]{0:T(512)} copy(f32[512]{0:T(512)S(1)} %bitcast.13) | data formatting | bytes 4096

commit v6 on v5

--- a/solution.py
+++ b/solution.py
@@ -444,7 +444,7 @@
                 pltpu.VMEM((tokens, width), BF16),
                 pltpu.VMEM((tokens, CH), BF16),
                 pltpu.VMEM((CH, tokens), BF16),
-                pltpu.VMEM((2 * tokens, CH), F32),
+                pltpu.VMEM((2 * tokens + 8, CH), F32),
                 pltpu.VMEM((4, CH, CH), F32),
                 pltpu.VMEM((tokens, CH), BF16),
                 pltpu.VMEM((tokens, CH), BF16),

time: 45.8 us -> 45.8 us (level)
  no operation moved by 1% of the time
where the time goes in v6:
time: 45.8 us; the launch traced here: 45.7 us
  Pallas kernels  41.8 us (91%)
  between operations  2.33 us (5%)
  local copies, waits for them, and re-layouts  1.55 us (3%)
    pallas_call x1, Pallas kernels, per_device(): pl.pallas_call(functools.partial(kernel, ns, nh), out_shape=(pltpu.VMEM((...  41.8 us
    unnamed x2, local copies, waits for them, and re-layouts  1.55 us

profile of v6, /device:TPU:1, one launch (start us, length us, event | category | flops | bytes accessed | tf_op | source)
XLA Modules:
  0.0 45.7 jit_solution(8553272483014738065)
XLA Ops:
  0.6 41.8 %shard_map.157 = (bf16[512,1024]{1,0:T(8,128)(2,1)S(1)}, f32[1,512]{1,0:T(1,128)S(1)}, f32[1,1]{1,0:T(1,128)}) custom-call(bf16[512,1024]{1,0:T(8,128)(2,1)} %refs_0_.1, bf16[512,1024]{1,0:T(8,128)(2,1)} %refs_1_.1, bf16[1024,128]{1,0:T(8,128)(2,1)} %bitcast.14, f32[16,512]{1,0:T(8,128)} %bitcast.15, f32[1,16]{1,0:T(1,128)} %bitcast.20, f32[1,16]{1,0:T(1,128)} %bitcast.21, ...), custom_call_target="tpu_custom_call" | custom-call | tf_op jit(solution)/shard_map/pallas_call | solution.py:433
  42.4 1.0 %copy.20 = bf16[512,1024]{1,0:T(8,128)(2,1)} copy(bf16[512,1024]{1,0:T(8,128)(2,1)S(1)} %get-tuple-element.9) | data formatting | bytes 2097152
  43.4 0.6 %copy.21 = f32[512]{0:T(512)} copy(f32[512]{0:T(512)S(1)} %bitcast.13) | data formatting | bytes 4096
